TPU v7x, 256 devices: a whole 4x4x8 slice. The times are simulated.
256 devices in a mesh: grp: 4 (over y), tok: 32 (over z, x_lo, core), ch: 2 (over x_hi).
Axes of the slice: x: 4 (x_hi: 2, x_lo: 2; x = x_hi * 2 + x_lo), y: 4, z: 8, core: 2. Of those that a mesh axis runs over, the one named last changes fastest.
Arguments:
- tokens: bfloat16 [512, 512, 1024], P(('grp', 'tok'), None, 'ch'), may hold values from -6 to 6
- row_factor: bfloat16 [512, 512, 512], P(('grp', 'tok')), may hold values from -0.25 to 0.25
- column_factor: bfloat16 [512, 512, 512], P(('grp', 'tok')), may hold values from -0.25 to 0.25
- kernel: bfloat16 [3, 3, 1024], P(None, None, 'ch'), may hold values from -2 to 2
- cotangent: bfloat16 [512, 512, 1024], P(('grp', 'tok'), None, 'ch'), may hold values from -6 to 6
Outputs:
- grad_tokens: bfloat16 [512, 512, 1024], P(('grp', 'tok'), None, 'ch')
- grad_row: bfloat16 [512, 512, 512], P(('grp', 'tok'), 'ch')
- grad_column: bfloat16 [512, 512, 512], P(('grp', 'tok'), 'ch')
- grad_kernel: float32 [3, 3, 1024], P(None, None, 'ch')
All inputs are finite; a program needn't handle non-finite values.
Results may differ from a plain program's by a relative error of at most 0.0058.
Values may be sent and summed in bfloat16 or wider, within the bound.
A program may use at most 128 MiB of HBM per device.

v0:
```python
import jax
import jax.numpy as jnp
from jax import lax
from jax.sharding import PartitionSpec as P


def extended(cells, sides, width):
    for axis, dim in sides:
        count = lax.axis_size(axis)
        ends = count - 1
        head = lax.slice_in_dim(cells, 0, width, axis=dim)
        tail = lax.slice_in_dim(cells, cells.shape[dim] - width, cells.shape[dim], axis=dim)
        cells = jnp.concatenate(
            [
                lax.ppermute(tail, axis, [(i, (i + 1) % count) for i in range(ends)]),
                cells,
                lax.ppermute(head, axis, [((i + 1) % count, i) for i in range(ends)]),
            ],
            axis=dim,
        )
    return cells


def to_columns(local):
    return lax.all_to_all(local, ("grp", "tok"), split_axis=1, concat_axis=0, tiled=True)


def to_rows(local):
    return lax.all_to_all(local, ("grp", "tok"), split_axis=0, concat_axis=1, tiled=True)


def shards(tokens, row_factor, column_factor, kernel, cotangent):
    rows, cols, chans = tokens.shape
    mixed_rows = jnp.einsum(
        "rce,red->rcd", row_factor, tokens, preferred_element_type=jnp.float32
    ).astype(jnp.bfloat16)
    rows_cols = to_columns(mixed_rows)
    mixed_cols = jnp.einsum(
        "crs,scd->rcd", column_factor, rows_cols, preferred_element_type=jnp.float32
    ).astype(jnp.bfloat16)
    mixed = to_rows(mixed_cols)
    gate = jax.nn.sigmoid(tokens.astype(jnp.float32))
    mixed_f = mixed.astype(jnp.float32)
    gated = (mixed_f * gate).astype(jnp.bfloat16)
    cot_rim = extended(cotangent, ((("grp", "tok"), 0),), 1)
    cot_pad = jnp.pad(cot_rim, ((0, 0), (1, 1), (0, 0))).astype(jnp.float32)
    cot_f = cotangent.astype(jnp.float32)
    kern_f = kernel.astype(jnp.float32)
    grad_gated = jnp.zeros((rows, cols, chans), jnp.float32)
    for i in range(3):
        for j in range(3):
            grad_gated = (
                grad_gated + kern_f[i, j] * cot_pad[2 - i : 2 - i + rows, 2 - j : 2 - j + cols]
            )
    kernel_rows = []
    gated_rim = extended(gated, ((("grp", "tok"), 0),), 1)
    gated_pad = jnp.pad(gated_rim, ((0, 0), (1, 1), (0, 0))).astype(jnp.float32)
    for i in range(3):
        kernel_cols = []
        for j in range(3):
            kernel_cols.append(jnp.sum(gated_pad[i : i + rows, j : j + cols] * cot_f, axis=(0, 1)))
        kernel_rows.append(jnp.stack(kernel_cols))
    grad_kernel = lax.psum(jnp.stack(kernel_rows), ("grp", "tok"))
    grad_mixed = (grad_gated * gate).astype(jnp.bfloat16)
    grad_gate_in = grad_gated * mixed_f * gate * (1.0 - gate)
    grad_cols = to_columns(grad_mixed)
    grad_rows_cols = jnp.einsum(
        "crs,rcd->scd", column_factor, grad_cols, preferred_element_type=jnp.float32
    ).astype(jnp.bfloat16)
    column_terms = jnp.einsum(
        "rcd,scd->crs", grad_cols, rows_cols, preferred_element_type=jnp.float32
    )
    grad_column = lax.psum_scatter(column_terms, "ch", scatter_dimension=1, tiled=True).astype(
        jnp.bfloat16
    )
    grad_rows = to_rows(grad_rows_cols)
    row_terms = jnp.einsum("rcd,red->rce", grad_rows, tokens, preferred_element_type=jnp.float32)
    grad_row = lax.psum_scatter(row_terms, "ch", scatter_dimension=1, tiled=True).astype(
        jnp.bfloat16
    )
    back_mixed = jnp.einsum(
        "rce,rcd->red", row_factor, grad_rows, preferred_element_type=jnp.float32
    )
    grad_tokens = (back_mixed + grad_gate_in).astype(jnp.bfloat16)
    return (grad_tokens, grad_row, grad_column, grad_kernel)


def solution(mesh):
    return jax.shard_map(
        shards,
        mesh=mesh,
        in_specs=(
            P(("grp", "tok"), None, "ch"),
            P(("grp", "tok"), None, None),
            P(("grp", "tok"), None, None),
            P(None, None, "ch"),
            P(("grp", "tok"), None, "ch"),
        ),
        out_specs=(
            P(("grp", "tok"), None, "ch"),
            P(("grp", "tok"), "ch", None),
            P(("grp", "tok"), "ch", None),
            P(None, None, "ch"),
        ),
        check_vma=False,
    )
```

profile of v0, /device:TPU:1, one launch (start us, length us, event | category | flops | bytes accessed | tf_op | source)
XLA Modules:
  0.0 912.9 jit_solution(4310347412737254671)
XLA Ops:
  13.8 15.3 %all-to-all-start.2 = ((bf16[4,512,512]{2,0,1:T(4,128)(2,1)}), bf16[4,512,512]{2,0,1:T(4,128)(2,1)}, u32[]{:S(2)}, u32[]{:S(2)}) async-start(bf16[4,512,512]{2,0,1:T(4,128)(2,1)} %copy.53), calls=%async_computation.2 | async-start | bytes 4194304 | tf_op jit(solution)/shard_map/all_to_all | solution.py:25
  44.3 6.1 collective-permute-done.1
  54.2 8.9 multiply_convert_fusion.1
  63.1 4.5 copy.47
  67.6 11.3 %all-to-all-done.2 = bf16[4,512,512]{2,0,1:T(4,128)(2,1)} async-done(((bf16[4,512,512]{2,0,1:T(4,128)(2,1)}), bf16[4,512,512]{2,0,1:T(4,128)(2,1)}, u32[]{:S(2)}, u32[]{:S(2)}) %all-to-all-start.2) | async-done | bytes 2097184 | tf_op jit(solution)/shard_map/all_to_all | solution.py:25
  78.9 31.2 %all-to-all-start = ((bf16[4,512,512]{2,0,1:T(4,128)(2,1)}), bf16[4,512,512]{2,0,1:T(4,128)(2,1)}, u32[]{:S(2)}, u32[]{:S(2)}) async-start(bf16[4,512,512]{2,0,1:T(4,128)(2,1)} %copy.47), calls=%async_computation | async-start | bytes 4194304 | tf_op jit(solution)/shard_map/all_to_all | solution.py:25
  110.4 4.2 copy.54
  114.6 45.3 %all-to-all-done = bf16[4,512,512]{2,0,1:T(4,128)(2,1)} async-done(((bf16[4,512,512]{2,0,1:T(4,128)(2,1)}), bf16[4,512,512]{2,0,1:T(4,128)(2,1)}, u32[]{:S(2)}, u32[]{:S(2)}) %all-to-all-start) | async-done | bytes 2097184 | tf_op jit(solution)/shard_map/all_to_all | solution.py:25
  167.7 4.2 convert_bitcast_fusion.2
  172.0 4.5 copy.50
  176.4 9.3 %all-to-all-start.1 = ((bf16[512,4,512]{2,1,0:T(4,128)(2,1)}), bf16[512,4,512]{2,1,0:T(4,128)(2,1)}, u32[]{:S(2)}, u32[]{:S(2)}) async-start(bf16[512,4,512]{2,1,0:T(4,128)(2,1)} %copy.50), calls=%async_computation.1 | async-start | bytes 4194304 | tf_op jit(solution)/shard_map/all_to_all | solution.py:29
  185.7 4.6 convert_bitcast_fusion.1
  190.3 4.5 copy.56
  194.9 40.7 %all-to-all-done.1 = bf16[512,4,512]{2,1,0:T(4,128)(2,1)} async-done(((bf16[512,4,512]{2,1,0:T(4,128)(2,1)}), bf16[512,4,512]{2,1,0:T(4,128)(2,1)}, u32[]{:S(2)}, u32[]{:S(2)}) %all-to-all-start.1) | async-done | bytes 2097184 | tf_op jit(solution)/shard_map/all_to_all | solution.py:29
  235.5 8.8 all-to-all-start.3
  252.4 42.1 %all-to-all-done.3 = bf16[512,4,512]{2,1,0:T(4,128)(2,1)S(1)} async-done(((bf16[512,4,512]{2,1,0:T(4,128)(2,1)}), bf16[512,4,512]{2,1,0:T(4,128)(2,1)S(1)}, u32[]{:S(2)}, u32[]{:S(2)}) %all-to-all-start.3) | async-done | bytes 2097184 | tf_op jit(solution)/shard_map/all_to_all | solution.py:29
  299.2 5.5 copy.58
  309.6 4.5 collective-permute-start.3
  316.5 5.3 fusion.18
  321.8 4.3 copy.64
  326.1 7.8 collective-permute-done.3
  334.0 5.3 fusion.19
  339.3 18.7 %fusion.1 = (f32[512]{0:T(512)S(1)}, f32[512]{0:T(512)S(1)}, f32[512]{0:T(512)S(1)}, f32[512]{0:T(512)S(1)}, f32[512]{0:T(512)S(1)}, /*index=5*/f32[512]{0:T(512...) fusion(bf16[4,512,512]{1,2,0:T(8,128)(2,1)S(1)} %copy-done.2, f32[6,514,512]{1,2,0:T(8,128)} %fusion.19), kind=kLoop, calls=%fused_computation.12 | loop fusion | flops 19918336 | bytes 39864320 | tf_op jit(solution)/shard_map/reduce_sum | solution.py:61
  358.1 542.4 %psum.7 = f32[3,3,512]{2,1,0:T(4,128)} all-reduce(f32[3,3,512]{2,1,0:T(4,128)S(1)} %pad_maximum_fusion), channel_id=1, replica_groups=mesh['grp'=4,'tok'=32,'ch'=2] {'grp','tok'}, use_global_device_ids=true, to_apply=%region_11.12 | all-reduce | flops 4608 | bytes 36864 | tf_op jit(solution)/shard_map/psum | solution.py:63
  (61 shorter events, 58.9 us)
Async XLA Ops:
  7.2 160.5 %copy-start = (bf16[4,512,512]{2,1,0:T(8,128)(2,1)S(1)}, bf16[4,512,512]{2,1,0:T(8,128)(2,1)}, u32[]{:S(2)}) copy-start(bf16[4,512,512]{2,1,0:T(8,128)(2,1)} %param.7) | copy-start | bytes 6291460
  13.8 65.2 %all-to-all-start.2 = ((bf16[4,512,512]{2,0,1:T(4,128)(2,1)}), bf16[4,512,512]{2,0,1:T(4,128)(2,1)}, u32[]{:S(2)}, u32[]{:S(2)}) async-start(bf16[4,512,512]{2,0,1:T(4,128)(2,1)} %copy.53), calls=%async_computation.2 | async-start | bytes 4194304 | tf_op jit(solution)/shard_map/all_to_all | solution.py:25
  33.3 11.0 %copy-start.14 = (bf16[3,3,512]{2,1,0:T(4,128)(2,1)S(1)}, bf16[3,3,512]{2,1,0:T(4,128)(2,1)}, u32[]{:S(2)}) copy-start(bf16[3,3,512]{2,1,0:T(4,128)(2,1)} %param.8) | copy-start | bytes 27652
  34.6 15.9 %collective-permute-start.1 = (bf16[1,512,512]{1,2,0:T(8,128)(2,1)S(1)}, bf16[1,512,512]{1,2,0:T(8,128)(2,1)}, u32[]{:S(2)}, u32[]{:S(2)}) collective-permute-start(bf16[1,512,512]{1,2,0:T(8,128)(2,1)S(1)} %get-tuple-element.30), channel_id=1, source_target_pairs={{2,0},{4,2},{6,4},{8,6},{10,8},{12,10},{14,12},{16,14},{18,16},{20... | collective-permute-start | bytes 1572872 | tf_op jit(solution)/shard_map/ppermute | solution.py:17
  37.5 13.0 %collective-permute-start = (bf16[1,512,512]{1,2,0:T(8,128)(2,1)S(1)}, bf16[1,512,512]{1,2,0:T(8,128)(2,1)}, u32[]{:S(2)}, u32[]{:S(2)}) collective-permute-start(bf16[1,512,512]{1,2,0:T(8,128)(2,1)S(1)} %get-tuple-element.29), channel_id=1, source_target_pairs={{0,2},{2,4},{4,6},{6,8},{8,10},{10,12},{12,14},{14,16},{16,18},{18... | collective-permute-start | bytes 1572872 | tf_op jit(solution)/shard_map/ppermute | solution.py:15
  44.3 9.9 %copy-start.3 = (bf16[4,512,512]{1,2,0:T(8,128)(2,1)S(1)}, bf16[4,512,512]{1,2,0:T(8,128)(2,1)}, u32[]{:S(2)}) copy-start(bf16[4,512,512]{1,2,0:T(8,128)(2,1)} %copy.46) | copy-start | bytes 6291460
  78.9 81.0 %all-to-all-start = ((bf16[4,512,512]{2,0,1:T(4,128)(2,1)}), bf16[4,512,512]{2,0,1:T(4,128)(2,1)}, u32[]{:S(2)}, u32[]{:S(2)}) async-start(bf16[4,512,512]{2,0,1:T(4,128)(2,1)} %copy.47), calls=%async_computation | async-start | bytes 4194304 | tf_op jit(solution)/shard_map/all_to_all | solution.py:25
  110.1 790.4 %reduce-scatter.5.cloned.1.call-start = ((), (), s32[]{:S(2)}) async-start(), calls=%async_computation.7 | async-start | bytes 6291456 | tf_op jit(solution)/shard_map/reduce_scatter | solution.py:73
  159.9 4.3 copy-start.6
  162.9 1.3 copy-start.7
  176.4 59.1 %all-to-all-start.1 = ((bf16[512,4,512]{2,1,0:T(4,128)(2,1)}), bf16[512,4,512]{2,1,0:T(4,128)(2,1)}, u32[]{:S(2)}, u32[]{:S(2)}) async-start(bf16[512,4,512]{2,1,0:T(4,128)(2,1)} %copy.50), calls=%async_computation.1 | async-start | bytes 4194304 | tf_op jit(solution)/shard_map/all_to_all | solution.py:29
  235.5 59.0 %all-to-all-start.3 = ((bf16[512,4,512]{2,1,0:T(4,128)(2,1)}), bf16[512,4,512]{2,1,0:T(4,128)(2,1)S(1)}, u32[]{:S(2)}, u32[]{:S(2)}) async-start(bf16[512,4,512]{2,1,0:T(4,128)(2,1)} %copy.56), calls=%async_computation.3 | async-start | bytes 4194304 | tf_op jit(solution)/shard_map/all_to_all | solution.py:29
  244.4 658.9 %reduce-scatter.3.cloned.1.call-start = ((), (), s32[]{:S(2)}) async-start(), calls=%async_computation.6 | async-start | bytes 6291456 | tf_op jit(solution)/shard_map/reduce_scatter | solution.py:78
  244.9 4.3 copy-start.10
  299.2 5.5 copy-start.4
  304.7 11.8 %copy-start.5 = (f32[4,512,512]{1,2,0:T(8,128)S(1)}, f32[4,512,512]{1,2,0:T(8,128)}, u32[]{:S(2)}) copy-start(f32[4,512,512]{1,2,0:T(8,128)} %copy.58) | copy-start | bytes 12582916
  304.7 11.8 %copy-start.12 = (bf16[4,128,4,512]{3,0,2,1:T(4,128)(2,1)S(1)}, bf16[4,128,4,512]{3,0,2,1:T(4,128)(2,1)}, u32[]{:S(2)}) copy-start(bf16[4,128,4,512]{3,0,2,1:T(4,128)(2,1)} %copy-done.11) | copy-start | bytes 6291460
  304.7 11.8 %copy-start.13 = (f32[4,512,512]{1,2,0:T(8,128)S(1)}, f32[4,512,512]{1,2,0:T(8,128)}, u32[]{:S(2)}) copy-start(f32[4,512,512]{1,2,0:T(8,128)} %get-tuple-element.26) | copy-start | bytes 12582916
  308.2 1.4 copy-start.8
  309.6 24.4 %collective-permute-start.3 = (bf16[1,512,512]{1,2,0:T(8,128)(2,1)S(1)}, bf16[1,512,512]{1,2,0:T(8,128)(2,1)}, u32[]{:S(2)}, u32[]{:S(2)}) collective-permute-start(bf16[1,512,512]{1,2,0:T(8,128)(2,1)S(1)} %get-tuple-element.28), channel_id=1, source_target_pairs={{2,0},{4,2},{6,4},{8,6},{10,8},{12,10},{14,12},{16,14},{18,16},{20... | collective-permute-start | bytes 1572872 | tf_op jit(solution)/shard_map/ppermute | solution.py:17
  314.1 19.8 %collective-permute-start.2 = (bf16[1,512,512]{1,2,0:T(8,128)(2,1)S(1)}, bf16[1,512,512]{1,2,0:T(8,128)(2,1)}, u32[]{:S(2)}, u32[]{:S(2)}) collective-permute-start(bf16[1,512,512]{1,2,0:T(8,128)(2,1)S(1)} %get-tuple-element.27), channel_id=1, source_target_pairs={{0,2},{2,4},{4,6},{6,8},{8,10},{10,12},{12,14},{14,16},{16,18},{18... | collective-permute-start | bytes 1572872 | tf_op jit(solution)/shard_map/ppermute | solution.py:15
  321.8 12.1 %copy-start.9 = (bf16[4,512,512]{1,2,0:T(8,128)(2,1)S(1)}, bf16[4,512,512]{1,2,0:T(8,128)(2,1)}, u32[]{:S(2)}) copy-start(bf16[4,512,512]{1,2,0:T(8,128)(2,1)} %copy-done.8) | copy-start | bytes 6291460
  326.1 13.2 %copy-start.2 = (bf16[4,512,512]{1,2,0:T(8,128)(2,1)S(1)}, bf16[4,512,512]{1,2,0:T(8,128)(2,1)}, u32[]{:S(2)}) copy-start(bf16[4,512,512]{1,2,0:T(8,128)(2,1)} %copy.43) | copy-start | bytes 6291460
  339.3 566.6 %copy-start.1 = (bf16[4,512,512]{2,1,0:T(8,128)(2,1)S(1)}, bf16[4,512,512]{2,1,0:T(8,128)(2,1)}, u32[]{:S(2)}) copy-start(bf16[4,512,512]{2,1,0:T(8,128)(2,1)} %param.7) | copy-start | bytes 6291460
  (1 other events, 1.3 us)
Sparse Core Ops, SparseCore 0:
  167.8 80.8 reduce-scatter.4
  252.6 81.2 reduce-scatter.2
where the time goes:
time: 927 us; the launch traced here: 913 us
  blocking collectives  542 us (58%)
  waiting for transfers between devices  153 us (17%)
  starting transfers between devices  77.8 us (8%)
  local copies, waits for them, and re-layouts  54.1 us (6%)
  other arithmetic  46.2 us (5%)
  matrix products  24.5 us (3%)
  between operations  14.5 us (2%)
    psum x1, blocking collectives, shards(): grad_kernel = lax.psum(jnp.stack(kernel_rows), ('grp', 'tok'))  542 us
    all_to_all x2, waiting for transfers between devices, to_rows(): lax.all_to_all(local, ('grp', 'tok'), split_axis=0, concat_axis=1, tiled=...  82.8 us
    all_to_all x2, waiting for transfers between devices, to_columns(): lax.all_to_all(local, ('grp', 'tok'), split_axis=1, concat_axis=0, tiled=...  56.6 us
    all_to_all x2, starting transfers between devices, to_columns(): lax.all_to_all(local, ('grp', 'tok'), split_axis=1, concat_axis=0, tiled=...  46.5 us
    reduce_sum x1, other arithmetic, shards(): jnp.sum(gated_pad[i:i + rows, j:j + cols] * cot_f, axis=(0, 1))  18.7 us
  transfers between devices with their start and end apart: 10, of which 6 were waited for; matrix products, arithmetic and copies ran while one was open for 12% of the time, Pallas kernels for 0%

commit v1 on v0

v1 whole, which is shorter than its diff:
```python
import functools

import jax
import jax.numpy as jnp
from jax import lax
from jax.experimental import pallas as pl
from jax.experimental.pallas import tpu as pltpu
from jax.sharding import PartitionSpec as P

MESH = pl.DeviceIdType.MESH
GRP, TOK = 4, 32
N = GRP * TOK


def place():
    return lax.axis_index("grp") * TOK + lax.axis_index("tok")


def device(t):
    return (t // TOK, lax.rem(t, TOK), lax.axis_index("ch"))


def exchange_kernel(count, *refs):
    srcs, dsts, (send_sem, recv_sem) = refs[:count], refs[count : 2 * count], refs[2 * count :]
    me = place()
    barrier = pltpu.get_barrier_semaphore()

    def greet(i, carry):
        t = lax.rem(me + i, N)
        pl.semaphore_signal(barrier, inc=1, device_id=device(t), device_id_type=MESH)
        return carry

    lax.fori_loop(1, N, greet, 0)
    pl.semaphore_wait(barrier, N - 1)
    for k in range(count):
        pltpu.make_async_copy(srcs[k].at[me], dsts[k].at[me], recv_sem.at[k]).start()

        def send(i, carry):
            t = lax.rem(me + i, N)
            pltpu.make_async_remote_copy(
                src_ref=srcs[k].at[t],
                dst_ref=dsts[k].at[me],
                send_sem=send_sem.at[k],
                recv_sem=recv_sem.at[k],
                device_id=device(t),
                device_id_type=MESH,
            ).start()
            return carry

        lax.fori_loop(1, N, send, 0)
    for k in range(count):
        pltpu.make_async_copy(
            srcs[k].at[pl.ds(0, N - 1)], dsts[k].at[pl.ds(0, N - 1)], send_sem.at[k]
        ).wait()
        pltpu.make_async_copy(srcs[k], dsts[k], recv_sem.at[k]).wait()


def exchange(call_id, *arrays):
    count = len(arrays)
    spec = pl.BlockSpec(memory_space=pltpu.VMEM)
    return pl.pallas_call(
        functools.partial(exchange_kernel, count),
        out_shape=[jax.ShapeDtypeStruct(a.shape, a.dtype) for a in arrays],
        in_specs=[spec] * count,
        out_specs=[spec] * count,
        scratch_shapes=[pltpu.SemaphoreType.DMA((count,)), pltpu.SemaphoreType.DMA((count,))],
        name="exchange",
        compiler_params=pltpu.CompilerParams(
            collective_id=call_id, has_side_effects=True, vmem_limit_bytes=24 * 2**20
        ),
    )(*arrays)


def sum_kernel(x_ref, o_ref, held, send_sem, recv_sem):
    y, tok, h = lax.axis_index("grp"), lax.axis_index("tok"), lax.axis_index("ch")
    z, xc = tok // 4, lax.rem(tok, 4)
    steps = (
        (8, lambda i: (y, lax.rem(z + i, 8) * 4 + xc, h)),
        (4, lambda i: (lax.rem(y + i, 4), tok, h)),
        (4, lambda i: (y, z * 4 + lax.rem(xc + i, 4), h)),
    )
    barrier = pltpu.get_barrier_semaphore()
    for size, peer in steps:
        for i in range(1, size):
            pl.semaphore_signal(barrier, inc=1, device_id=peer(i), device_id_type=MESH)
    pl.semaphore_wait(barrier, 13)
    o_ref[...] = x_ref[...]
    slot = 0
    for k, (size, peer) in enumerate(steps):
        for i in range(1, size):
            pltpu.make_async_remote_copy(
                src_ref=o_ref,
                dst_ref=held.at[slot + i - 1],
                send_sem=send_sem.at[k],
                recv_sem=recv_sem.at[k],
                device_id=peer(i),
                device_id_type=MESH,
            ).start()
        span = held.at[pl.ds(slot, size - 1)]
        pltpu.make_async_copy(span, span, send_sem.at[k]).wait()
        pltpu.make_async_copy(span, span, recv_sem.at[k]).wait()
        o_ref[...] = o_ref[...] + jnp.sum(held[slot : slot + size - 1], axis=0)
        slot += size - 1


def sum_cells(x):
    spec = pl.BlockSpec(memory_space=pltpu.VMEM)
    return pl.pallas_call(
        sum_kernel,
        out_shape=jax.ShapeDtypeStruct(x.shape, x.dtype),
        in_specs=[spec],
        out_specs=spec,
        scratch_shapes=[
            pltpu.VMEM((13,) + x.shape, x.dtype),
            pltpu.SemaphoreType.DMA((3,)),
            pltpu.SemaphoreType.DMA((3,)),
        ],
        name="sum_cells",
        compiler_params=pltpu.CompilerParams(collective_id=7, has_side_effects=True),
    )(x)


def rim(cells):
    perm = [(i, i + 1) for i in range(N - 1)]
    back = [(i + 1, i) for i in range(N - 1)]
    return jnp.concatenate(
        [
            lax.ppermute(cells[-1:], ("grp", "tok"), perm),
            cells,
            lax.ppermute(cells[:1], ("grp", "tok"), back),
        ],
        axis=0,
    )


def pack(local):
    rows, cols, chans = local.shape
    return local.reshape(rows, N, cols // N, chans).transpose(1, 0, 2, 3).reshape(N, -1, chans)


def shards(tokens, row_factor, column_factor, kernel, cotangent):
    rows, cols, chans = tokens.shape
    wide = cols // N
    mixed_rows = jnp.einsum(
        "rce,red->rcd", row_factor, tokens, preferred_element_type=jnp.float32
    ).astype(jnp.bfloat16)
    gate = jax.nn.sigmoid(tokens.astype(jnp.float32))
    cot_pad = jnp.pad(rim(cotangent), ((0, 0), (1, 1), (0, 0))).astype(jnp.float32)
    kern_f = kernel.astype(jnp.float32)
    grad_gated = jnp.zeros((rows, cols, chans), jnp.float32)
    for i in range(3):
        for j in range(3):
            grad_gated = (
                grad_gated + kern_f[i, j] * cot_pad[2 - i : 2 - i + rows, 2 - j : 2 - j + cols]
            )
    grad_mixed = (grad_gated * gate).astype(jnp.bfloat16)
    got_mixed, got_grad = exchange(1, pack(mixed_rows), pack(grad_mixed))

    def columns(got):
        return got.reshape(N, rows, wide, chans).transpose(2, 0, 1, 3).reshape(wide, N * rows, chans)

    col_mixed, col_grad = columns(got_mixed), columns(got_grad)
    mixed_cols = jnp.einsum(
        "crs,csd->crd", column_factor, col_mixed, preferred_element_type=jnp.float32
    ).astype(jnp.bfloat16)
    grad_cols = jnp.einsum(
        "crs,crd->csd", column_factor, col_grad, preferred_element_type=jnp.float32
    ).astype(jnp.bfloat16)
    column_terms = jnp.einsum(
        "crd,csd->crs", col_grad, col_mixed, preferred_element_type=jnp.float32
    )
    grad_column = lax.psum_scatter(column_terms, "ch", scatter_dimension=1, tiled=True).astype(
        jnp.bfloat16
    )

    def unpack_columns(local):
        return (
            local.reshape(wide, N, rows, chans).transpose(1, 2, 0, 3).reshape(N, rows * wide, chans)
        )

    back_mixed, back_grad = exchange(2, unpack_columns(mixed_cols), unpack_columns(grad_cols))

    def by_rows(got):
        return got.reshape(N, rows, wide, chans).transpose(1, 0, 2, 3).reshape(rows, cols, chans)

    mixed, grad_rows = by_rows(back_mixed), by_rows(back_grad)
    mixed_f = mixed.astype(jnp.float32)
    gated = (mixed_f * gate).astype(jnp.bfloat16).astype(jnp.float32)
    kernel_rows = []
    for i in range(3):
        for j in range(3):
            kernel_rows.append(
                jnp.sum(gated * cot_pad[2 - i : 2 - i + rows, 2 - j : 2 - j + cols], axis=(0, 1))
            )
    grad_kernel = sum_cells(jnp.pad(jnp.stack(kernel_rows), ((0, 7), (0, 0))))
    grad_kernel = grad_kernel[:9].reshape(3, 3, chans)
    grad_gate_in = grad_gated * mixed_f * gate * (1.0 - gate)
    row_terms = jnp.einsum("rcd,red->rce", grad_rows, tokens, preferred_element_type=jnp.float32)
    grad_row = lax.psum_scatter(row_terms, "ch", scatter_dimension=1, tiled=True).astype(
        jnp.bfloat16
    )
    back = jnp.einsum("rce,rcd->red", row_factor, grad_rows, preferred_element_type=jnp.float32)
    grad_tokens = (back + grad_gate_in).astype(jnp.bfloat16)
    return (grad_tokens, grad_row, grad_column, grad_kernel)


def solution(mesh):
    return jax.shard_map(
        shards,
        mesh=mesh,
        in_specs=(
            P(("grp", "tok"), None, "ch"),
            P(("grp", "tok"), None, None),
            P(("grp", "tok"), None, None),
            P(None, None, "ch"),
            P(("grp", "tok"), None, "ch"),
        ),
        out_specs=(
            P(("grp", "tok"), None, "ch"),
            P(("grp", "tok"), "ch", None),
            P(("grp", "tok"), "ch", None),
            P(None, None, "ch"),
        ),
        check_vma=False,
    )
```

time: 927 us -> 415 us (0.45); the launches traced: 913 us -> 413 us
  blocking collectives: 542 us -> 0 us
  Pallas kernels: 0 us -> 225 us
  waiting for transfers between devices: 153 us -> 0.04 us
  starting transfers between devices: 77.8 us -> 7.51 us
  local copies, waits for them, and re-layouts: 54.1 us -> 97.5 us
    psum x1 -> x0, blocking collectives: 542 us -> none  [shards(): grad_kernel = lax.psum(jnp.stack(kernel_rows), ('grp', 'tok'))]
    pallas_call x0 -> x3, Pallas kernels: none -> 225 us  [the longest x2 204 us: exchange(): pl.pallas_call(functools.partial(exchange_kernel, count), out_shape=[jax....]
    all_to_all x4 -> x0, waiting for transfers between devices: 139 us -> none  [the longest x2 82.8 us: to_rows(): lax.all_to_all(local, ('grp', 'tok'), split_axis=0, concat_axis=1, tiled=...]
    all_to_all x4 -> x0, starting transfers between devices: 64.6 us -> none  [the longest x2 46.5 us: to_columns(): lax.all_to_all(local, ('grp', 'tok'), split_axis=1, concat_axis=0, tiled=...]
    reshape x0 -> x13, local copies, waits for them, and re-layouts: none -> 45.8 us  [the longest x4 16 us: pack(): local.reshape(rows, N, cols // N, chans).transpose(1, 0, 2, 3)]
    ppermute x4 -> x2, waiting for transfers between devices: 14 us -> 0.01 us  [the longest x1 0.01 us: rim(): lax.ppermute(cells[:1], ('grp', 'tok'), back)]
    convert_element_type x3 -> x0, local copies, waits for them, and re-layouts: 12 us -> none  [the longest x1 4.53 us: shards(): mixed_cols = jnp.einsum('crs,scd->rcd', column_factor, rows_cols, preferr...]
    all_to_all x3 -> x0, local copies, waits for them, and re-layouts: 10.1 us -> none  [the longest x2 7.18 us: to_columns(): lax.all_to_all(local, ('grp', 'tok'), split_axis=1, concat_axis=0, tiled=...]
  transfers between devices with their start and end apart: 10 -> 4, of which waited for: 6 -> 0; matrix products, arithmetic and copies ran while one was open for 12% -> 26% of each run, Pallas kernels for 0% -> 29%
where the time goes in v1:
time: 415 us; the launch traced here: 413 us
  Pallas kernels  225 us (54%)
  local copies, waits for them, and re-layouts  97.5 us (23%)
  other arithmetic  38.9 us (9%)
  matrix products  30 us (7%)
  between operations  14.2 us (3%)
  starting transfers between devices  7.51 us (2%)
    pallas_call x2, Pallas kernels, exchange(): pl.pallas_call(functools.partial(exchange_kernel, count), out_shape=[jax....  204 us
    unnamed x35, local copies, waits for them, and re-layouts  24.3 us
    pallas_call x1, Pallas kernels, sum_cells(): pl.pallas_call(sum_kernel, out_shape=jax.ShapeDtypeStruct(x.shape, x.dtyp...  21.4 us
    reduce_sum x1, other arithmetic, shards(): jnp.sum(gated * cot_pad[2 - i:2 - i + rows, 2 - j:2 - j + cols], axis=(0,...  20.8 us
    reshape x4, local copies, waits for them, and re-layouts, pack(): local.reshape(rows, N, cols // N, chans).transpose(1, 0, 2, 3)  16 us
    convert_element_type x3, local copies, waits for them, and re-layouts, shards(): mixed_f = mixed.astype(jnp.float32)  14.7 us
    reshape x4, local copies, waits for them, and re-layouts, unpack_columns(): local.reshape(wide, N, rows, chans).transpose(1, 2, 0, 3)  13.8 us
    convert_element_type x1, other arithmetic, shards(): grad_mixed = (grad_gated * gate).astype(jnp.bfloat16)  8.82 us
  transfers between devices with their start and end apart: 4, of which 0 were waited for; matrix products, arithmetic and copies ran while one was open for 26% of the time, Pallas kernels for 29%

profile of v1, /device:TPU:1, one launch (start us, length us, event | category | flops | bytes accessed | tf_op | source)
XLA Modules:
  0.0 413.4 jit_solution(10588486797723514721)
XLA Ops:
  7.2 4.3 %copy.25 = bf16[4,512,512]{1,2,0:T(8,128)(2,1)} copy(bf16[4,512,512]{2,1,0:T(8,128)(2,1)} %param.9) | data formatting | bytes 4194304 | tf_op args[4]
  12.8 4.5 %collective-permute-start = (bf16[1,512,512]{1,2,0:T(8,128)(2,1)S(1)}, bf16[1,512,512]{1,2,0:T(8,128)(2,1)}, u32[]{:S(2)}, u32[]{:S(2)}) collective-permute-start(bf16[1,512,512]{1,2,0:T(8,128)(2,1)S(1)} %get-tuple-element.31), channel_id=1, source_target_pairs={{0,2},{2,4},{4,6},{6,8},{8,10},{10,12},{12,14},{14,16},{16,18},{18... | collective-permute-start | bytes 1572872 | tf_op jit(solution)/shard_map/ppermute | solution.py:128
  20.0 4.1 %copy.28 = bf16[4,512,512]{1,2,0:T(8,128)(2,1)} copy(bf16[4,512,512]{2,1,0:T(8,128)(2,1)} %param.5) | data formatting | bytes 4194304 | tf_op args[0]
  24.2 4.8 %convolution_convert_fusion = bf16[4,512,512]{2,1,0:T(8,128)(2,1)} fusion(bf16[4,512,512]{2,1,0:T(8,128)(2,1)} %param.6, bf16[4,512,512]{2,1,0:T(8,128)(2,1)} %param.5), kind=kOutput, calls=%fused_computation.36 | convolution fusion | flops 1074790400 | bytes 6291456 | tf_op jit(solution)/shard_map/rce,red->rcd/dot_general | solution.py:144
  28.9 4.0 reshape.59
  32.9 4.1 copy.57
  45.0 8.8 %multiply_convert_fusion.1 = (bf16[4,512,512]{1,2,0:T(8,128)(2,1)}, f32[4,512,512]{1,2,0:T(8,128)}) fusion(bf16[4,512,512]{1,2,0:T(8,128)(2,1)S(1)} %copy-done.12, f32[6,514,512]{1,2,0:T(8,128)S(1)} %fusion.16, f32[512]{0:T(512)S(1)} %bitcast.76, f32[512]{0:T(512)S(1)} %bitcast.75, f32[512]{0:T(512)S(1)} %bitcast.74, f32[512]{0:T(512)S(1)} %bitcast.73, ...), kind=kLoop, calls=%fused_computation.27 | loop fusion | flops 24117248 | bytes 46155776 | tf_op jit(solution)/shard_map/convert_element_type | solution.py:156
  53.8 4.5 %copy.29 = bf16[4,512,512]{2,0,1:T(4,128)(2,1)} copy(bf16[4,512,512]{1,2,0:T(8,128)(2,1)} %get-tuple-element.29) | data formatting | bytes 4194304 | tf_op jit(solution)/shard_map/convert_element_type | solution.py:156
  58.3 4.1 %copy.30 = bf16[128,4,4,512]{3,2,1,0:T(4,128)(2,1)} copy(bf16[128,4,4,512]{3,1,2,0:T(4,128)(2,1)} %bitcast.63) | data formatting | bytes 4194304 | tf_op jit(solution)/shard_map/transpose | solution.py:138
  69.5 104.6 %exchange.2 = (bf16[128,16,512]{2,1,0:T(8,128)(2,1)S(1)}, bf16[128,16,512]{2,1,0:T(8,128)(2,1)S(1)}) custom-call(bf16[128,16,512]{2,1,0:T(8,128)(2,1)S(1)} %copy-done.2, bf16[128,16,512]{2,1,0:T(8,128)(2,1)S(1)} %copy-done.4), custom_call_target="tpu_custom_call" | custom-call | tf_op jit(solution)/shard_map/exchange/pallas_call | solution.py:61
  176.9 4.0 reshape.63
  180.9 4.0 reshape.67
  184.9 5.6 %fusion.17 = f32[4,512,512]{2,1,0:T(8,128)} fusion(bf16[4,512,512]{2,0,1:T(4,128)(2,1)} %bitcast.58, bf16[4,512,512]{2,0,1:T(4,128)(2,1)} %bitcast.60), kind=kOutput, calls=%fused_computation.37 | convolution fusion | flops 1073741824 | bytes 8388608 | tf_op jit(solution)/shard_map/crd,csd->crs/dot_general | solution.py:169
  196.6 4.0 reshape.66.refs_0_
  207.0 4.0 reshape.70.refs_1_
  212.6 99.2 %exchange.3 = (bf16[128,16,512]{2,1,0:T(8,128)(2,1)S(1)}, bf16[128,16,512]{2,1,0:T(8,128)(2,1)S(1)}) custom-call(bf16[128,16,512]{2,1,0:T(8,128)(2,1)S(1)} %copy-done.3, bf16[128,16,512]{2,1,0:T(8,128)(2,1)S(1)} %copy-done.5), custom_call_target="tpu_custom_call" | custom-call | tf_op jit(solution)/shard_map/exchange/pallas_call | solution.py:61
  319.0 4.1 reshape.72
  323.1 4.8 %fusion.24 = f32[4,512,512]{2,1,0:T(8,128)} fusion(bf16[4,512,512]{2,1,0:T(8,128)(2,1)} %reshape.72, bf16[4,512,512]{2,1,0:T(8,128)(2,1)S(1)} %copy-done.14), kind=kOutput, calls=%fused_computation.44 | convolution fusion | flops 1073741824 | bytes 8388608 | tf_op jit(solution)/shard_map/rcd,red->rce/dot_general | solution.py:198
  332.5 6.3 %copy.38 = f32[128,4,4,512]{3,1,2,0:T(4,128)} copy(f32[128,4,4,512]{3,2,1,0:T(4,128)} %reshape.75) | data formatting | bytes 8388608 | tf_op jit(solution)/shard_map/convert_element_type | solution.py:187
  338.8 5.4 %copy.39 = f32[4,512,512]{1,2,0:T(8,128)} copy(f32[4,512,512]{2,0,1:T(4,128)} %bitcast.57) | data formatting | bytes 8388608 | tf_op jit(solution)/shard_map/convert_element_type | solution.py:187
  344.3 8.4 %fusion.13 = bf16[4,512,512]{1,2,0:T(8,128)(2,1)} fusion(f32[4,512,512]{1,2,0:T(8,128)} %get-tuple-element.30, f32[4,512,512]{1,2,0:T(8,128)} %copy.39, bf16[4,512,512]{2,1,0:T(8,128)(2,1)} %reshape.72, bf16[4,512,512]{2,1,0:T(8,128)(2,1)} %param.6, bf16[4,512,512]{1,2,0:T(8,128)(2,1)S(1)} %copy-done.13), kind=kOutput, calls=%fused_computation.25 | convolution fusion | flops 1084227584 | bytes 16777216 | tf_op jit(solution)/shard_map/rce,rcd->red/dot_general | solution.py:202
  352.7 4.1 %copy.41 = bf16[4,512,512]{2,1,0:T(8,128)(2,1)} copy(bf16[4,512,512]{1,2,0:T(8,128)(2,1)} %fusion.13) | data formatting | bytes 4194304
  356.9 20.8 %fusion.12 = (f32[512]{0:T(512)S(1)}, f32[512]{0:T(512)S(1)}, f32[512]{0:T(512)S(1)}, f32[512]{0:T(512)S(1)}, f32[512]{0:T(512)S(1)}, /*index=5*/f32[512]{0:T(51...) fusion(f32[6,514,512]{1,2,0:T(8,128)} %copy-done.11, f32[4,512,512]{1,2,0:T(8,128)} %copy.39, ...), kind=kLoop, calls=%fused_computation.23 | loop fusion | flops 26209792 | bytes 44058624 | tf_op jit(solution)/shard_map/reduce_sum | solution.py:193
  378.3 21.4 %sum_cells.1 = f32[16,512]{1,0:T(8,128)} custom-call(f32[16,512]{1,0:T(8,128)} %pad.9.x_ref), custom_call_target="tpu_custom_call" | custom-call | tf_op jit(solution)/shard_map/sum_cells/pallas_call | solution.py:108
  (58 shorter events, 55.1 us)
Async XLA Ops:
  7.2 183.6 %copy-start = (bf16[4,512,512]{2,1,0:T(8,128)(2,1)S(1)}, bf16[4,512,512]{2,1,0:T(8,128)(2,1)}, u32[]{:S(2)}) copy-start(bf16[4,512,512]{2,1,0:T(8,128)(2,1)} %param.7) | copy-start | bytes 6291460
  7.2 394.0 %reduce-scatter.5.cloned.1.call-start = ((), (), s32[]{:S(2)}) async-start(), calls=%async_computation.3 | async-start | bytes 6291456 | tf_op jit(solution)/shard_map/reduce_scatter | solution.py:172
  12.8 28.2 %collective-permute-start = (bf16[1,512,512]{1,2,0:T(8,128)(2,1)S(1)}, bf16[1,512,512]{1,2,0:T(8,128)(2,1)}, u32[]{:S(2)}, u32[]{:S(2)}) collective-permute-start(bf16[1,512,512]{1,2,0:T(8,128)(2,1)S(1)} %get-tuple-element.31), channel_id=1, source_target_pairs={{0,2},{2,4},{4,6},{6,8},{8,10},{10,12},{12,14},{14,16},{16,18},{18... | collective-permute-start | bytes 1572872 | tf_op jit(solution)/shard_map/ppermute | solution.py:128
  17.3 23.7 %collective-permute-start.1 = (bf16[1,512,512]{1,2,0:T(8,128)(2,1)S(1)}, bf16[1,512,512]{1,2,0:T(8,128)(2,1)}, u32[]{:S(2)}, u32[]{:S(2)}) collective-permute-start(bf16[1,512,512]{1,2,0:T(8,128)(2,1)S(1)} %get-tuple-element.32), channel_id=1, source_target_pairs={{2,0},{4,2},{6,4},{8,6},{10,8},{12,10},{14,12},{16,14},{18,16},{20... | collective-permute-start | bytes 1572872 | tf_op jit(solution)/shard_map/ppermute | solution.py:130
  32.9 8.1 %copy-start.15 = (bf16[3,3,512]{2,1,0:T(4,128)(2,1)S(1)}, bf16[3,3,512]{2,1,0:T(4,128)(2,1)}, u32[]{:S(2)}) copy-start(bf16[3,3,512]{2,1,0:T(4,128)(2,1)} %param.8) | copy-start | bytes 27652
  41.0 4.0 copy-start.12
  44.9 8.8 %copy-start.11 = (f32[6,514,512]{1,2,0:T(8,128)}, f32[6,514,512]{1,2,0:T(8,128)S(1)}, u32[]{:S(2)}) copy-start(f32[6,514,512]{1,2,0:T(8,128)S(1)} %fusion.16) | copy-start | bytes 18948100
  66.4 1.6 copy-start.2
  67.9 1.6 copy-start.4
  174.2 1.4 copy-start.8
  175.6 1.3 copy-start.9
  190.5 213.3 %reduce-scatter.3.cloned.1.call-start = ((), (), s32[]{:S(2)}) async-start(), calls=%async_computation.2 | async-start | bytes 6291456 | tf_op jit(solution)/shard_map/reduce_scatter | solution.py:199
  204.0 6.9 %copy-start.3 = (bf16[128,16,512]{2,1,0:T(8,128)(2,1)S(1)}, bf16[128,16,512]{2,1,0:T(8,128)(2,1)}, u32[]{:S(2)}) copy-start(bf16[128,16,512]{2,1,0:T(8,128)(2,1)} %reshape.66.refs_0_) | copy-start | bytes 6291460
  210.9 1.7 copy-start.5
  311.8 1.3 copy-start.6
  313.1 1.3 copy-start.10
  319.0 4.1 copy-start.14
  327.9 1.6 copy-start.7
  338.8 5.4 %copy-start.13 = (bf16[4,512,512]{1,2,0:T(8,128)(2,1)S(1)}, bf16[4,512,512]{1,2,0:T(8,128)(2,1)}, u32[]{:S(2)}) copy-start(bf16[4,512,512]{1,2,0:T(8,128)(2,1)} %copy.28) | copy-start | bytes 6291460
  356.9 49.7 %copy-start.1 = (bf16[4,512,512]{2,1,0:T(8,128)(2,1)S(1)}, bf16[4,512,512]{2,1,0:T(8,128)(2,1)}, u32[]{:S(2)}) copy-start(bf16[4,512,512]{2,1,0:T(8,128)(2,1)} %param.7) | copy-start | bytes 6291460
Sparse Core Ops, SparseCore 0:
  190.6 93.2 reduce-scatter.4
  328.1 59.3 reduce-scatter.2

commit v2 on v0

v2 whole, which is shorter than its diff:
```python
import jax
import jax.numpy as jnp
from jax import lax
from jax.experimental import pallas as pl
from jax.experimental.pallas import tpu as pltpu
from jax.sharding import PartitionSpec as P

MESH = pl.DeviceIdType.MESH
F32, BF16 = jnp.float32, jnp.bfloat16
Y, Z, XC = 4, 8, 4
N = Y * Z * XC
ROWS = 4
SIZE = 512
CELL = ROWS * ROWS
BAND = SIZE // Y
EDGE = 16
STEP = 128


def dot(a, b, contract=((1,), (0,))):
    return lax.dot_general(a, b, (contract, ((), ())), preferred_element_type=F32)


def aligned(value, multiple):
    return pl.multiple_of(value, multiple)


def mixer(
    tok_h, rf_h, cf_h, kern, cot_h,
    gtok_h, grow_h, gcol_h, gkern,
    tok, rf, cf, cotp, s1, s2, r1, r2, r3, r4, xs, gs, hold, mid, grows,
    row_out, col_out, row_got, col_got, row_done, col_done, taps, kf, total, held, t1, t2,
    load_sem, halo_send, halo_recv, send_sem, recv_sem, last_sem,
    col_send, col_recv, row_send, row_recv, sum_send, sum_recv, store_sem,
):
    y, tk, h = lax.axis_index("grp"), lax.axis_index("tok"), lax.axis_index("ch")
    z, xc = tk // XC, lax.rem(tk, XC)
    me = y * (Z * XC) + tk
    other = (y, tk, 1 - h)

    def device(t):
        return (t // (Z * XC), lax.rem(t, Z * XC), h)

    loads = [
        pltpu.make_async_copy(tok_h, tok, load_sem.at[0]),
        pltpu.make_async_copy(rf_h, rf, load_sem.at[1]),
        pltpu.make_async_copy(cot_h, cotp.at[pl.ds(1, ROWS), pl.ds(EDGE, SIZE), :], load_sem.at[2]),
        pltpu.make_async_copy(cf_h, cf, load_sem.at[3]),
    ]
    for load in loads:
        load.start()

    barrier = pltpu.get_barrier_semaphore()

    def greet(i, carry):
        pl.semaphore_signal(
            barrier, inc=1, device_id=device(lax.rem(me + i, N)), device_id_type=MESH
        )
        return carry

    lax.fori_loop(1, N, greet, 0)
    pl.semaphore_signal(barrier, inc=1, device_id=other, device_id_type=MESH)

    out = lax.broadcasted_iota(jnp.int32, (256, 256), 0)
    src = lax.broadcasted_iota(jnp.int32, (256, 256), 1)
    first, second, third = out >> 4, (out >> 2) & 3, out & 3
    t1[...] = (src == second * 64 + first * 4 + third).astype(F32).astype(BF16)
    first, second, third = out >> 6, (out >> 2) & 15, out & 3
    t2[...] = (src == second * 16 + third * 4 + first).astype(F32).astype(BF16)
    cotp[:, 0:EDGE, :] = jnp.zeros((ROWS + 2, EDGE, SIZE), BF16)
    cotp[:, EDGE + SIZE :, :] = jnp.zeros((ROWS + 2, EDGE, SIZE), BF16)
    for i in range(3):
        kf[3 * i : 3 * i + 3, :] = kern[i].astype(F32)
    taps[...] = jnp.zeros_like(taps)

    up, down = lax.rem(me + N - 1, N), lax.rem(me + 1, N)
    halos = [
        pltpu.make_async_remote_copy(
            src_ref=cot_h.at[ROWS - 1],
            dst_ref=cotp.at[0, pl.ds(EDGE, SIZE), :],
            send_sem=halo_send.at[0],
            recv_sem=halo_recv.at[0],
            device_id=device(down),
            device_id_type=MESH,
        ),
        pltpu.make_async_remote_copy(
            src_ref=cot_h.at[0],
            dst_ref=cotp.at[ROWS + 1, pl.ds(EDGE, SIZE), :],
            send_sem=halo_send.at[1],
            recv_sem=halo_recv.at[1],
            device_id=device(up),
            device_id_type=MESH,
        ),
    ]

    def pack(band, parts, buf):
        for half in range(2):
            stack = jnp.concatenate([p[64 * half : 64 * half + 64] for p in parts], axis=0)
            at = aligned(band * (Z * XC * CELL) + half * 256, 256)
            buf[pl.ds(at, 256), :] = dot(t1[...], stack).astype(BF16)

    def send(dy, buf, dst, k, sems):
        band = lax.rem(y + dy, Y)
        mine = aligned(me * CELL, CELL)

        @pl.when(dy == 0)
        def _():
            pltpu.make_async_copy(
                buf.at[pl.ds(mine, CELL), :], dst.at[pl.ds(mine, CELL), :], sems(0)
            ).start()

        def one(i, carry):
            par = i // 16
            dz = lax.rem(i // 4, 4) * 2 + par
            t = band * (Z * XC) + lax.rem(z + dz, Z) * XC + lax.rem(xc + i, XC)
            pltpu.make_async_remote_copy(
                src_ref=buf.at[pl.ds(aligned(t * CELL, CELL), CELL), :],
                dst_ref=dst.at[pl.ds(mine, CELL), :],
                send_sem=send_sem.at[k],
                recv_sem=sems(dy * 2 + par),
                device_id=device(t),
                device_id_type=MESH,
            ).start()
            return carry

        lax.fori_loop(jnp.where(dy == 0, 1, 0), Z * XC, one, 0)

    def wait_sent(buf, k):
        part = buf.at[pl.ds(0, (N - 1) * CELL), :]
        pltpu.make_async_copy(part, part, send_sem.at[k]).wait()

    def wait_got(buf, k):
        pltpu.make_async_copy(buf, buf, recv_sem.at[k]).wait()

    def unpack(buf, dst):
        def one(b, carry):
            block = dot(t2[...], buf[pl.ds(aligned(b * 256, 256), 256), :]).astype(BF16)
            for w in range(ROWS):
                dst[w, pl.ds(aligned(b * 64, 64), 64), :] = block[64 * w : 64 * w + 64]
            return carry

        lax.fori_loop(0, N * CELL // 256, one, 0)

    def band_of(dy):
        band = lax.rem(y + dy, Y)
        return band, pl.ds(aligned(band * BAND, BAND), BAND)

    loads[0].wait()
    loads[1].wait()

    def mix_rows(dy, carry):
        band, cols = band_of(dy)
        pack(band, [dot(rf[q, cols, :], tok[q]).astype(BF16) for q in range(ROWS)], s1)

        @pl.when(dy == 0)
        def _():
            pl.semaphore_wait(barrier, N)
            for halo in halos:
                halo.start()

        send(dy, s1, r1, 0, lambda g: recv_sem.at[0])
        return carry

    lax.fori_loop(0, Y, mix_rows, 0)

    loads[2].wait()
    for halo in halos:
        halo.wait_recv()

    @pl.when(me == 0)
    def _():
        cotp[0, EDGE : EDGE + SIZE, :] = jnp.zeros((SIZE, SIZE), BF16)

    @pl.when(me == N - 1)
    def _():
        cotp[ROWS + 1, EDGE : EDGE + SIZE, :] = jnp.zeros((SIZE, SIZE), BF16)

    parts = SIZE // STEP

    def tile(it):
        r = it // (parts * parts)
        at = aligned(lax.rem(it // parts, parts) * STEP, STEP)
        lanes = pl.ds(aligned(lax.rem(it, parts) * STEP, STEP), STEP)
        wide = pl.ds(at, STEP + 2 * EDGE)
        return r, pl.ds(at, STEP), wide, lanes

    inner = slice(EDGE, EDGE + STEP)
    span = STEP + 2 * EDGE

    def shifted(x):
        return (pltpu.roll(x, span - 1, 0)[inner], x[inner], pltpu.roll(x, 1, 0)[inner])

    def conv(it, carry):
        r, cols, wide, lanes = tile(it)
        rows = [cotp[r + 2 - i, wide, lanes].astype(F32) for i in range(3)]
        sums = []
        for j in range(3):
            term = rows[0] * kf[j : j + 1, lanes]
            for i in (1, 2):
                term = term + rows[i] * kf[3 * i + j : 3 * i + j + 1, lanes]
            sums.append(term)
        grad = (
            pltpu.roll(sums[0], span - 1, 0)[inner]
            + sums[1][inner]
            + pltpu.roll(sums[2], 1, 0)[inner]
        )
        gate = jax.nn.sigmoid(tok[r, cols, lanes].astype(F32))
        grad = grad * gate
        mid[r, cols, lanes] = grad.astype(BF16)
        hold[r, cols, lanes] = grad * (1.0 - gate)
        return carry

    lax.fori_loop(0, ROWS * parts * parts, conv, 0)

    def send_grad(dy, carry):
        band, cols = band_of(dy)
        pack(band, [mid[q, cols, :] for q in range(ROWS)], s2)
        send(dy, s2, r2, 1, lambda g: recv_sem.at[1])
        return carry

    lax.fori_loop(0, Y, send_grad, 0)

    loads[3].wait()
    wait_got(r1, 0)
    unpack(r1, xs)
    wait_sent(s1, 0)

    def mix_columns(dy, carry):
        band, cols = band_of(dy)
        pack(band, [dot(cf[q, cols, :], xs[q]).astype(BF16) for q in range(ROWS)], s1)
        send(dy, s1, r3, 2, lambda g: recv_sem.at[2])
        return carry

    lax.fori_loop(0, Y, mix_columns, 0)

    wait_got(r2, 1)
    unpack(r2, gs)
    wait_sent(s2, 1)

    def back_columns(dy, carry):
        band, cols = band_of(dy)
        pack(
            band,
            [dot(cf[q, :, cols], gs[q], ((0,), (0,))).astype(BF16) for q in range(ROWS)],
            s2,
        )
        send(dy, s2, r4, 3, lambda g: last_sem.at[g])
        return carry

    lax.fori_loop(0, Y, back_columns, 0)

    def half_of(which):
        return pl.ds(aligned(which * (SIZE // 2), SIZE // 2), SIZE // 2)

    def column_copy(q):
        return pltpu.make_async_remote_copy(
            src_ref=col_out.at[q],
            dst_ref=col_got.at[q],
            send_sem=col_send.at[q],
            recv_sem=col_recv.at[q],
            device_id=other,
            device_id_type=MESH,
        )

    def column_away(q, carry):
        col_out[q] = dot(gs[q, half_of(1 - h), :], xs[q], ((1,), (1,))).astype(BF16)
        column_copy(q).start()
        return carry

    lax.fori_loop(0, ROWS, column_away, 0)

    wait_got(r3, 2)
    unpack(r3, mid)

    def gated(it, carry):
        r, cols, wide, lanes = tile(it)
        mixed = mid[r, cols, lanes].astype(F32)
        gate = jax.nn.sigmoid(tok[r, cols, lanes].astype(F32))
        cells = (mixed * gate).astype(BF16).astype(F32)
        hold[r, cols, lanes] = hold[r, cols, lanes] * mixed
        for i in range(3):
            row = cotp[r + 2 - i, wide, lanes].astype(F32)
            for j, moved in enumerate(shifted(row)):
                term = (cells * moved).reshape(STEP // 8, 8, STEP)
                taps[3 * i + j, :, lanes] += jnp.sum(term, axis=0)
        return carry

    lax.fori_loop(0, ROWS * parts * parts, gated, 0)

    steps = (
        (Z, 0, lambda i: (y, lax.rem(z + i, Z) * XC + xc, h)),
        (Y, Z - 1, lambda i: (lax.rem(y + i, Y), tk, h)),
        (XC, Z + Y - 2, lambda i: (y, z * XC + lax.rem(xc + i, XC), h)),
    )

    def sum_start(k):
        size, slot, peer = steps[k]
        for i in range(1, size):
            pltpu.make_async_remote_copy(
                src_ref=total.at[k],
                dst_ref=held.at[slot + i - 1],
                send_sem=sum_send.at[k],
                recv_sem=sum_recv.at[k],
                device_id=peer(i),
                device_id_type=MESH,
            ).start()

    def sum_finish(k):
        size, slot, _ = steps[k]
        part = held.at[pl.ds(slot, size - 1)]
        pltpu.make_async_copy(part, part, sum_recv.at[k]).wait()
        total[k + 1] = total[k] + jnp.sum(held[slot : slot + size - 1], axis=0)

    def sum_sent(k):
        size, slot, _ = steps[k]
        part = held.at[pl.ds(slot, size - 1)]
        pltpu.make_async_copy(part, part, sum_send.at[k]).wait()

    total[0] = jnp.zeros((16, SIZE), F32)
    for k in range(9):
        total[0, k : k + 1, :] = jnp.sum(taps[k], axis=0, keepdims=True)
    sum_start(0)

    def column_store(q):
        return pltpu.make_async_copy(col_done.at[q], gcol_h.at[q], store_sem.at[q])

    def column_here(q, carry):
        term = dot(gs[q, half_of(h), :], xs[q], ((1,), (1,)))
        column_copy(q).wait_recv()
        col_done[q] = (term + col_got[q].astype(F32)).astype(BF16)
        column_store(q).start()
        return carry

    lax.fori_loop(0, ROWS, column_here, 0)
    sum_finish(0)
    sum_start(1)

    def source(dy):
        band = lax.rem(y + Y - dy, Y)
        return band, band // 2 != h, aligned(lax.rem(band, 2) * BAND, BAND)

    def row_copy(at):
        part = pl.ds(at, 16)
        return pltpu.make_async_remote_copy(
            src_ref=row_out.at[:, part, :],
            dst_ref=row_got.at[:, part, :],
            send_sem=row_send.at[at // BAND],
            recv_sem=row_recv.at[at // BAND],
            device_id=other,
            device_id_type=MESH,
        )

    def row_store(slot):
        part = pl.ds(slot * BAND, BAND)
        return pltpu.make_async_copy(
            row_done.at[:, part, :], grow_h.at[:, part, :], store_sem.at[ROWS + slot]
        )

    def row_here(dy):
        band, away, base = source(dy)

        @pl.when(jnp.logical_not(away))
        def _():
            part = pl.ds(base, BAND)
            got = row_got.at[:, part, :]
            pltpu.make_async_copy(got, got, row_recv.at[base // BAND]).wait()
            cols = pl.ds(aligned(band * BAND, BAND), BAND)
            for q in range(ROWS):
                term = dot(grows[q, cols, :], tok[q], ((1,), (1,)))
                row_done[q, part, :] = (term + row_got[q, part, :].astype(F32)).astype(BF16)
            row_store(base // BAND).start()

    def arrive(dy, carry):
        band, away, base = source(dy)
        for par in range(2):
            g = dy * 2 + par
            part = r4.at[pl.ds(0, 256), :]
            pltpu.make_async_copy(part, part, last_sem.at[g]).wait()
            zp = lax.rem(z + par, 2)
            blocks = [
                r4[pl.ds(aligned((band * Z + zp + 2 * m) * 64, 64), 64), :] for m in range(4)
            ]
            block = dot(t2[...], jnp.concatenate(blocks, axis=0)).astype(BF16)
            for q in range(ROWS):
                for m in range(4):
                    at = aligned(band * BAND + (zp + 2 * m) * 16, 16)
                    low = 64 * q + 16 * m
                    grows[q, pl.ds(at, 16), :] = block[low : low + 16]

            @pl.when(away)
            def _():
                for q in range(ROWS):
                    term = dot(block[64 * q : 64 * q + 64], tok[q], ((1,), (1,))).astype(BF16)
                    for m in range(4):
                        at = aligned(base + (zp + 2 * m) * 16, 16)
                        row_out[q, pl.ds(at, 16), :] = term[16 * m : 16 * m + 16]
                for m in range(4):
                    row_copy(aligned(base + (zp + 2 * m) * 16, 16)).start()

        cols = pl.ds(aligned(band * BAND, BAND), BAND)
        for q in range(ROWS):
            hold[q] = hold[q] + dot(rf[q, cols, :], grows[q, cols, :], ((0,), (0,)))

        @pl.when(dy > 0)
        def _():
            row_here(dy - 1)

        @pl.when(dy == 0)
        def _():
            sum_finish(1)
            sum_start(2)

        return carry

    lax.fori_loop(0, Y, arrive, 0)

    def token_store(q):
        return pltpu.make_async_copy(mid.at[q], gtok_h.at[q], store_sem.at[ROWS + 2 + q])

    def token_out(q, carry):
        mid[q] = hold[q].astype(BF16)
        token_store(q).start()
        return carry

    lax.fori_loop(0, ROWS, token_out, 0)
    sum_finish(2)
    for i in range(3):
        gkern[i] = total[3, 3 * i : 3 * i + 3, :]
    row_here(Y - 1)

    wait_sent(s1, 2)
    wait_sent(s2, 3)
    for halo in halos:
        halo.wait_send()
    for k in range(3):
        sum_sent(k)
    for slot in range(2):
        part = row_out.at[:, pl.ds(slot * BAND, BAND), :]
        pltpu.make_async_copy(part, part, row_send.at[slot]).wait()
        row_store(slot).wait()
    for q in range(ROWS):
        column_copy(q).wait_send()
        column_store(q).wait()
        token_store(q).wait()


def shards(tokens, row_factor, column_factor, kernel, cotangent):
    full = (ROWS, SIZE, SIZE)
    half = (ROWS, SIZE // 2, SIZE)
    flat = (N * CELL, SIZE)
    vmem, dma = pltpu.VMEM, pltpu.SemaphoreType.DMA
    whole = pl.BlockSpec(memory_space=pl.ANY)
    local = pl.BlockSpec(memory_space=pltpu.VMEM)
    return pl.pallas_call(
        mixer,
        out_shape=[
            jax.ShapeDtypeStruct(full, BF16),
            jax.ShapeDtypeStruct(half, BF16),
            jax.ShapeDtypeStruct(half, BF16),
            jax.ShapeDtypeStruct((3, 3, SIZE), F32),
        ],
        in_specs=[whole, whole, whole, local, whole],
        out_specs=[whole, whole, whole, local],
        scratch_shapes=[
            vmem(full, BF16), vmem(full, BF16), vmem(full, BF16),
            vmem((ROWS + 2, SIZE + 2 * EDGE, SIZE), BF16),
            vmem(flat, BF16), vmem(flat, BF16),
            vmem(flat, BF16), vmem(flat, BF16), vmem(flat, BF16), vmem(flat, BF16),
            vmem(full, BF16), vmem(full, BF16), vmem(full, F32), vmem(full, BF16), vmem(full, BF16),
            vmem(half, BF16), vmem(half, BF16), vmem(half, BF16), vmem(half, BF16),
            vmem(half, BF16), vmem(half, BF16),
            vmem((9, 8, SIZE), F32), vmem((16, SIZE), F32),
            vmem((4, 16, SIZE), F32), vmem((Z + Y + XC - 3, 16, SIZE), F32),
            vmem((256, 256), BF16), vmem((256, 256), BF16),
            dma((4,)), dma((2,)), dma((2,)), dma((4,)), dma((3,)), dma((2 * Y,)),
            dma((ROWS,)), dma((ROWS,)), dma((2,)), dma((2,)), dma((3,)), dma((3,)),
            dma((2 * ROWS + 2,)),
        ],
        name="mixer",
        compiler_params=pltpu.CompilerParams(
            collective_id=1, has_side_effects=True, vmem_limit_bytes=58 * 2**20
        ),
        cost_estimate=pl.CostEstimate(
            flops=7 * 10**9, bytes_accessed=12 * 2**20, transcendentals=4 * 10**6
        ),
    )(tokens, row_factor, column_factor, kernel, cotangent)


def solution(mesh):
    return jax.shard_map(
        lambda *args: tuple(shards(*args)),
        mesh=mesh,
        in_specs=(
            P(("grp", "tok"), None, "ch"),
            P(("grp", "tok"), None, None),
            P(("grp", "tok"), None, None),
            P(None, None, "ch"),
            P(("grp", "tok"), None, "ch"),
        ),
        out_specs=(
            P(("grp", "tok"), None, "ch"),
            P(("grp", "tok"), "ch", None),
            P(("grp", "tok"), "ch", None),
            P(None, None, "ch"),
        ),
        check_vma=False,
    )
```

time: 927 us -> 250 us (0.27)
  the two profiles are of different devices: /device:TPU:1 before, /device:TPU:44 now
where the time goes in v2:
time: 250 us
  Pallas kernels  243 us (97%)
  local copies, waits for them, and re-layouts  6.32 us (3%)
    pallas_call x1, Pallas kernels, shards(): pl.pallas_call(mixer, out_shape=[jax.ShapeDtypeStruct(full, BF16), jax.Sh...  243 us
    unnamed x10, local copies, waits for them, and re-layouts  6.32 us

profile of v2, /device:TPU:44, one launch (start us, length us, event | category | flops | bytes accessed | tf_op | source)
XLA Modules:
  0.0 250.3 jit_solution(9189099825763642153)
XLA Ops:
  0.6 243.3 %mixer.1 = (bf16[4,512,512]{2,1,0:T(8,128)(2,1)}, bf16[4,256,512]{2,1,0:T(8,128)(2,1)}, bf16[4,256,512]{2,1,0:T(8,128)(2,1)}, f32[3,3,512]{2,1,0:T(4,128)}) custom-call(bf16[4,512,512]{2,1,0:T(8,128)(2,1)} %tok_h.1, bf16[4,512,512]{2,1,0:T(8,128)(2,1)} %rf_h.1, bf16[4,512,512]{2,1,0:T(8,128)(2,1)} %cf_h.1, bf16[3,3,512]{2,1,0:T(4,128)(2,1)} %kern.1, ...), custom_call_target="tpu_custom_call" | custom-call | flops 7000000000 | bytes 12582912 | tf_op jit(solution)/shard_map/mixer/pallas_call | solution.py:454
  244.0 0.0 copy-start.1
  244.0 3.1 %copy.13 = bf16[4,512,512]{2,1,0:T(8,128)(2,1)} copy(bf16[4,512,512]{2,1,0:T(8,128)(2,1)} %get-tuple-element.8) | data formatting | bytes 4194304
  247.1 0.0 copy-done.1
  247.1 0.0 copy-start
  247.1 0.0 copy-start.2
  247.1 1.0 copy.14
  248.1 0.6 copy-done
  248.7 1.0 copy.15
  249.7 0.0 copy-done.2
  249.7 0.6 copy.16
Async XLA Ops:
  244.0 3.1 %copy-start.1 = (bf16[4,256,512]{2,1,0:T(8,128)(2,1)S(1)}, bf16[4,256,512]{2,1,0:T(8,128)(2,1)}, u32[]{:S(2)}) copy-start(bf16[4,256,512]{2,1,0:T(8,128)(2,1)} %get-tuple-element.9) | copy-start | bytes 3145732
  247.1 1.6 copy-start
  247.1 2.6 %copy-start.2 = (f32[3,3,512]{2,1,0:T(4,128)S(1)}, f32[3,3,512]{2,1,0:T(4,128)}, u32[]{:S(2)}) copy-start(f32[3,3,512]{2,1,0:T(4,128)} %get-tuple-element.11) | copy-start | bytes 55300

commit v3 on v2

--- a/solution.py
+++ b/solution.py
@@ -29,8 +29,8 @@
     tok_h, rf_h, cf_h, kern, cot_h,
     gtok_h, grow_h, gcol_h, gkern,
     tok, rf, cf, cotp, s1, s2, r1, r2, r3, r4, xs, gs, hold, mid, grows,
-    row_out, col_out, row_got, col_got, row_done, col_done, taps, kf, total, held, t1, t2,
-    load_sem, halo_send, halo_recv, send_sem, recv_sem, last_sem,
+    row_out, col_out, row_got, col_got, row_done, col_done, relay, taps, kf, total, held, t1, t2,
+    load_sem, halo_send, halo_recv, hand_send, hand_recv, pass_send, send_sem, recv_sem, last_sem,
     col_send, col_recv, row_send, row_recv, sum_send, sum_recv, store_sem,
 ):
     y, tk, h = lax.axis_index("grp"), lax.axis_index("tok"), lax.axis_index("ch")
@@ -47,7 +47,7 @@
         pltpu.make_async_copy(cot_h, cotp.at[pl.ds(1, ROWS), pl.ds(EDGE, SIZE), :], load_sem.at[2]),
         pltpu.make_async_copy(cf_h, cf, load_sem.at[3]),
     ]
-    for load in loads:
+    for load in loads[:2]:
         load.start()
 
     barrier = pltpu.get_barrier_semaphore()
@@ -65,33 +65,89 @@
     src = lax.broadcasted_iota(jnp.int32, (256, 256), 1)
     first, second, third = out >> 4, (out >> 2) & 3, out & 3
     t1[...] = (src == second * 64 + first * 4 + third).astype(F32).astype(BF16)
-    first, second, third = out >> 6, (out >> 2) & 15, out & 3
-    t2[...] = (src == second * 16 + third * 4 + first).astype(F32).astype(BF16)
-    cotp[:, 0:EDGE, :] = jnp.zeros((ROWS + 2, EDGE, SIZE), BF16)
-    cotp[:, EDGE + SIZE :, :] = jnp.zeros((ROWS + 2, EDGE, SIZE), BF16)
-    for i in range(3):
-        kf[3 * i : 3 * i + 3, :] = kern[i].astype(F32)
-    taps[...] = jnp.zeros_like(taps)
-
+    quarter = SIZE // XC
+    first_of_z = y * (Z * XC) + z * XC
     up, down = lax.rem(me + N - 1, N), lax.rem(me + 1, N)
-    halos = [
-        pltpu.make_async_remote_copy(
-            src_ref=cot_h.at[ROWS - 1],
-            dst_ref=cotp.at[0, pl.ds(EDGE, SIZE), :],
-            send_sem=halo_send.at[0],
-            recv_sem=halo_recv.at[0],
-            device_id=device(down),
+    up_z, down_z = lax.rem(first_of_z + N - 1, N), lax.rem(first_of_z + XC, N)
+    ways = (
+        (0, ROWS - 1, 0, XC - 1, down, down_z),
+        (1, 0, ROWS + 1, 0, up, up_z),
+    )
+
+    def halo_copy(way, source, cols, sem, to):
+        return pltpu.make_async_remote_copy(
+            src_ref=source,
+            dst_ref=cotp.at[ways[way][2], cols, :],
+            send_sem=sem,
+            recv_sem=halo_recv.at[way],
+            device_id=device(to),
             device_id_type=MESH,
-        ),
-        pltpu.make_async_remote_copy(
-            src_ref=cot_h.at[0],
-            dst_ref=cotp.at[ROWS + 1, pl.ds(EDGE, SIZE), :],
-            send_sem=halo_send.at[1],
-            recv_sem=halo_recv.at[1],
-            device_id=device(up),
+        )
+
+    def halo_whole(way):
+        _, row, _, _, to, _ = ways[way]
+        return halo_copy(way, cot_h.at[row], pl.ds(EDGE, SIZE), halo_send.at[way], to)
+
+    def halo_own(way):
+        _, row, _, end, to, _ = ways[way]
+        source = cot_h.at[row, pl.ds(end * quarter, quarter), :]
+        return halo_copy(way, source, pl.ds(EDGE + end * quarter, quarter), halo_send.at[way], to)
+
+    def halo_hand(way, k):
+        row = ways[way][1]
+        return pltpu.make_async_remote_copy(
+            src_ref=cot_h.at[row, pl.ds(k * quarter, quarter), :],
+            dst_ref=relay.at[way],
+            send_sem=hand_send.at[way],
+            recv_sem=hand_recv.at[way],
+            device_id=(y, z * XC + k, h),
             device_id_type=MESH,
-        ),
-    ]
+        )
+
+    def halo_pass(way):
+        cols = pl.ds(aligned(EDGE + xc * quarter, EDGE), quarter)
+        return halo_copy(way, relay.at[way], cols, pass_send.at[way], ways[way][5])
+
+    def halo_start():
+        for way, _, _, end, _, _ in ways:
+
+            @pl.when(xc == end)
+            def _():
+                for k in range(XC):
+                    if k != end:
+                        halo_hand(way, k).start()
+                halo_own(way).start()
+
+            @pl.when(xc != end)
+            def _():
+                halo_whole(way).start()
+
+    def halo_forward():
+        for way, _, _, end, _, _ in ways:
+
+            @pl.when(xc != end)
+            def _():
+                pltpu.make_async_copy(relay.at[way], relay.at[way], hand_recv.at[way]).wait()
+                halo_pass(way).start()
+
+    def halo_got():
+        for way, _, row, _, _, _ in ways:
+            part = cotp.at[row, pl.ds(EDGE, SIZE), :]
+            pltpu.make_async_copy(part, part, halo_recv.at[way]).wait()
+
+    def halo_sent():
+        for way, _, _, end, _, _ in ways:
+
+            @pl.when(xc == end)
+            def _():
+                part = cotp.at[0, pl.ds(EDGE, (XC - 1) * quarter), :]
+                pltpu.make_async_copy(part, part, hand_send.at[way]).wait()
+                halo_own(way).wait_send()
+
+            @pl.when(xc != end)
+            def _():
+                halo_whole(way).wait_send()
+                halo_pass(way).wait_send()
 
     def pack(band, parts, buf):
         for half in range(2):
@@ -145,27 +201,43 @@
         band = lax.rem(y + dy, Y)
         return band, pl.ds(aligned(band * BAND, BAND), BAND)
 
+    pl.semaphore_wait(barrier, N)
+    halo_start()
+
     loads[0].wait()
     loads[1].wait()
+    loads[2].start()
+    loads[3].start()
 
     def mix_rows(dy, carry):
         band, cols = band_of(dy)
         pack(band, [dot(rf[q, cols, :], tok[q]).astype(BF16) for q in range(ROWS)], s1)
-
-        @pl.when(dy == 0)
-        def _():
-            pl.semaphore_wait(barrier, N)
-            for halo in halos:
-                halo.start()
-
+        return carry
+
+    def send_rows(dy, carry):
         send(dy, s1, r1, 0, lambda g: recv_sem.at[0])
         return carry
 
-    lax.fori_loop(0, Y, mix_rows, 0)
+    mix_rows(jnp.int32(0), 0)
+    send_rows(jnp.int32(0), 0)
+    halo_forward()
+
+    def mix_and_send(dy, carry):
+        mix_rows(dy, carry)
+        return send_rows(dy, carry)
+
+    lax.fori_loop(1, Y, mix_and_send, 0)
+
+    first, second, third = out >> 6, (out >> 2) & 15, out & 3
+    t2[...] = (src == second * 16 + third * 4 + first).astype(F32).astype(BF16)
+    cotp[:, 0:EDGE, :] = jnp.zeros((ROWS + 2, EDGE, SIZE), BF16)
+    cotp[:, EDGE + SIZE :, :] = jnp.zeros((ROWS + 2, EDGE, SIZE), BF16)
+    for i in range(3):
+        kf[3 * i : 3 * i + 3, :] = kern[i].astype(F32)
+    taps[...] = jnp.zeros_like(taps)
 
     loads[2].wait()
-    for halo in halos:
-        halo.wait_recv()
+    halo_got()
 
     @pl.when(me == 0)
     def _():
@@ -244,10 +316,14 @@
             [dot(cf[q, :, cols], gs[q], ((0,), (0,))).astype(BF16) for q in range(ROWS)],
             s2,
         )
+        return carry
+
+    def send_back(dy, carry):
         send(dy, s2, r4, 3, lambda g: last_sem.at[g])
         return carry
 
     lax.fori_loop(0, Y, back_columns, 0)
+    lax.fori_loop(0, Y // 2, send_back, 0)
 
     def half_of(which):
         return pl.ds(aligned(which * (SIZE // 2), SIZE // 2), SIZE // 2)
@@ -320,6 +396,7 @@
     for k in range(9):
         total[0, k : k + 1, :] = jnp.sum(taps[k], axis=0, keepdims=True)
     sum_start(0)
+    lax.fori_loop(Y // 2, Y, send_back, 0)
 
     def column_store(q):
         return pltpu.make_async_copy(col_done.at[q], gcol_h.at[q], store_sem.at[q])
@@ -331,13 +408,10 @@
         column_store(q).start()
         return carry
 
-    lax.fori_loop(0, ROWS, column_here, 0)
-    sum_finish(0)
-    sum_start(1)
-
     def source(dy):
         band = lax.rem(y + Y - dy, Y)
-        return band, band // 2 != h, aligned(lax.rem(band, 2) * BAND, BAND)
+        cols = pl.ds(aligned(band * BAND, BAND), BAND)
+        return band, cols, band // 2 != h, aligned(lax.rem(band, 2) * BAND, BAND)
 
     def row_copy(at):
         part = pl.ds(at, 16)
@@ -357,81 +431,79 @@
         )
 
     def row_here(dy):
-        band, away, base = source(dy)
+        band, cols, away, base = source(dy)
 
         @pl.when(jnp.logical_not(away))
         def _():
             part = pl.ds(base, BAND)
             got = row_got.at[:, part, :]
+            terms = [dot(grows[q, cols, :], tok[q], ((1,), (1,))) for q in range(ROWS)]
             pltpu.make_async_copy(got, got, row_recv.at[base // BAND]).wait()
-            cols = pl.ds(aligned(band * BAND, BAND), BAND)
             for q in range(ROWS):
-                term = dot(grows[q, cols, :], tok[q], ((1,), (1,)))
-                row_done[q, part, :] = (term + row_got[q, part, :].astype(F32)).astype(BF16)
+                row_done[q, part, :] = (terms[q] + row_got[q, part, :].astype(F32)).astype(BF16)
             row_store(base // BAND).start()
 
-    def arrive(dy, carry):
-        band, away, base = source(dy)
-        for par in range(2):
-            g = dy * 2 + par
-            part = r4.at[pl.ds(0, 256), :]
-            pltpu.make_async_copy(part, part, last_sem.at[g]).wait()
-            zp = lax.rem(z + par, 2)
-            blocks = [
-                r4[pl.ds(aligned((band * Z + zp + 2 * m) * 64, 64), 64), :] for m in range(4)
-            ]
-            block = dot(t2[...], jnp.concatenate(blocks, axis=0)).astype(BF16)
+    def arrive(dy, par):
+        band, cols, away, base = source(dy)
+        g = dy * 2 + par
+        part = r4.at[pl.ds(0, 256), :]
+        pltpu.make_async_copy(part, part, last_sem.at[g]).wait()
+        zp = lax.rem(z + par, 2)
+        blocks = [r4[pl.ds(aligned((band * Z + zp + 2 * m) * 64, 64), 64), :] for m in range(4)]
+        block = dot(t2[...], jnp.concatenate(blocks, axis=0)).astype(BF16)
+        for q in range(ROWS):
+            for m in range(4):
+                at = aligned(band * BAND + (zp + 2 * m) * 16, 16)
+                low = 64 * q + 16 * m
+                grows[q, pl.ds(at, 16), :] = block[low : low + 16]
+
+        @pl.when(away)
+        def _():
             for q in range(ROWS):
+                term = dot(block[64 * q : 64 * q + 64], tok[q], ((1,), (1,))).astype(BF16)
                 for m in range(4):
-                    at = aligned(band * BAND + (zp + 2 * m) * 16, 16)
-                    low = 64 * q + 16 * m
-                    grows[q, pl.ds(at, 16), :] = block[low : low + 16]
-
-            @pl.when(away)
-            def _():
-                for q in range(ROWS):
-                    term = dot(block[64 * q : 64 * q + 64], tok[q], ((1,), (1,))).astype(BF16)
-                    for m in range(4):
-                        at = aligned(base + (zp + 2 * m) * 16, 16)
-                        row_out[q, pl.ds(at, 16), :] = term[16 * m : 16 * m + 16]
-                for m in range(4):
-                    row_copy(aligned(base + (zp + 2 * m) * 16, 16)).start()
-
-        cols = pl.ds(aligned(band * BAND, BAND), BAND)
+                    at = aligned(base + (zp + 2 * m) * 16, 16)
+                    row_out[q, pl.ds(at, 16), :] = term[16 * m : 16 * m + 16]
+            for m in range(4):
+                row_copy(aligned(base + (zp + 2 * m) * 16, 16)).start()
+
+    def back(dy, q):
+        cols = source(dy)[1]
+        return hold[q] + dot(rf[q, cols, :], grows[q, cols, :], ((0,), (0,)))
+
+    def token_store(q):
+        return pltpu.make_async_copy(mid.at[q], gtok_h.at[q], store_sem.at[ROWS + 2 + q])
+
+    for dy in range(Y):
+        arrive(dy, 0)
+        if dy == 3:
+            row_here(0)
+        arrive(dy, 1)
         for q in range(ROWS):
-            hold[q] = hold[q] + dot(rf[q, cols, :], grows[q, cols, :], ((0,), (0,)))
-
-        @pl.when(dy > 0)
-        def _():
-            row_here(dy - 1)
-
-        @pl.when(dy == 0)
-        def _():
+            if dy < 3:
+                hold[q] = back(dy, q)
+            else:
+                mid[q] = back(dy, q).astype(BF16)
+                token_store(q).start()
+        if dy == 0:
+            lax.fori_loop(0, ROWS, column_here, 0)
+        if dy == 1:
+            sum_finish(0)
+            sum_start(1)
+        if dy == 2:
             sum_finish(1)
             sum_start(2)
-
-        return carry
-
-    lax.fori_loop(0, Y, arrive, 0)
-
-    def token_store(q):
-        return pltpu.make_async_copy(mid.at[q], gtok_h.at[q], store_sem.at[ROWS + 2 + q])
-
-    def token_out(q, carry):
-        mid[q] = hold[q].astype(BF16)
-        token_store(q).start()
-        return carry
-
-    lax.fori_loop(0, ROWS, token_out, 0)
-    sum_finish(2)
-    for i in range(3):
-        gkern[i] = total[3, 3 * i : 3 * i + 3, :]
-    row_here(Y - 1)
+        if dy == 3:
+            row_here(1)
+            row_here(2)
+            sum_finish(2)
+            for i in range(3):
+                gkern[i] = total[3, 3 * i : 3 * i + 3, :]
+            row_here(3)
 
     wait_sent(s1, 2)
     wait_sent(s2, 3)
-    for halo in halos:
-        halo.wait_send()
+    halo_sent()
     for k in range(3):
         sum_sent(k)
     for slot in range(2):
@@ -469,16 +541,16 @@
             vmem(full, BF16), vmem(full, BF16), vmem(full, F32), vmem(full, BF16), vmem(full, BF16),
             vmem(half, BF16), vmem(half, BF16), vmem(half, BF16), vmem(half, BF16),
             vmem(half, BF16), vmem(half, BF16),
-            vmem((9, 8, SIZE), F32), vmem((16, SIZE), F32),
+            vmem((2, SIZE // XC, SIZE), BF16), vmem((9, 8, SIZE), F32), vmem((16, SIZE), F32),
             vmem((4, 16, SIZE), F32), vmem((Z + Y + XC - 3, 16, SIZE), F32),
             vmem((256, 256), BF16), vmem((256, 256), BF16),
-            dma((4,)), dma((2,)), dma((2,)), dma((4,)), dma((3,)), dma((2 * Y,)),
+            dma((4,)), dma((2,)), dma((2,)), dma((2,)), dma((2,)), dma((2,)), dma((4,)), dma((3,)), dma((2 * Y,)),
             dma((ROWS,)), dma((ROWS,)), dma((2,)), dma((2,)), dma((3,)), dma((3,)),
             dma((2 * ROWS + 2,)),
         ],
         name="mixer",
         compiler_params=pltpu.CompilerParams(
-            collective_id=1, has_side_effects=True, vmem_limit_bytes=58 * 2**20
+            collective_id=1, has_side_effects=True, vmem_limit_bytes=49 * 2**20
         ),
         cost_estimate=pl.CostEstimate(
             flops=7 * 10**9, bytes_accessed=12 * 2**20, transcendentals=4 * 10**6

time: 250 us -> 229 us (0.916)
  the two profiles are of different devices: /device:TPU:44 before, /device:TPU:25 now
where the time goes in v3:
time: 229 us
  Pallas kernels  224 us (98%)
  local copies, waits for them, and re-layouts  4.57 us (2%)
    pallas_call x1, Pallas kernels, shards(): pl.pallas_call(mixer, out_shape=[jax.ShapeDtypeStruct(full, BF16), jax.Sh...  224 us

profile of v3, /device:TPU:25, one launch (start us, length us, event | category | flops | bytes accessed | tf_op | source)
XLA Modules:
  0.0 228.7 jit_solution(4988631277571718772)
XLA Ops:
  0.6 0.0 copy-start
  0.6 0.7 copy-done
  1.3 223.5 %mixer.1 = (bf16[4,512,512]{2,1,0:T(8,128)(2,1)S(1)}, bf16[4,256,512]{2,1,0:T(8,128)(2,1)S(1)}, bf16[4,256,512]{2,1,0:T(8,128)(2,1)S(1)}, f32[3,3,512]{2,1,0:T(4,128)S(1)}) custom-call(bf16[4,512,512]{2,1,0:T(8,128)(2,1)} %tok_h.1, bf16[4,512,512]{2,1,0:T(8,128)(2,1)} %rf_h.1, bf16[4,512,512]{2,1,0:T(8,128)(2,1)} %cf_h.1, bf16[3,3,512]{2,1,0:T(4,128)(2,1)S(1)} %copy-done, ...), custom_call_target="tpu_custom_call" | custom-call | flops 7000000000 | bytes 12582912 | tf_op jit(solution)/shard_map/mixer/pallas_call | solution.py:526
  224.9 1.3 copy.13
  226.2 1.0 copy.14
  227.2 1.0 copy.15
  228.1 0.6 copy.16
Async XLA Ops:
  0.6 0.7 copy-start

commit v4 on v3

--- a/solution.py
+++ b/solution.py
@@ -29,7 +29,7 @@
     tok_h, rf_h, cf_h, kern, cot_h,
     gtok_h, grow_h, gcol_h, gkern,
     tok, rf, cf, cotp, s1, s2, r1, r2, r3, r4, xs, gs, hold, mid, grows,
-    row_out, col_out, row_got, col_got, row_done, col_done, relay, taps, kf, total, held, t1, t2,
+    row_out, col_out, row_got, col_got, row_done, col_done, relay, taps, kf, total, held, t1, t2, t3,
     load_sem, halo_send, halo_recv, hand_send, hand_recv, pass_send, send_sem, recv_sem, last_sem,
     col_send, col_recv, row_send, row_recv, sum_send, sum_recv, store_sem,
 ):
@@ -39,7 +39,7 @@
     other = (y, tk, 1 - h)
 
     def device(t):
-        return (t // (Z * XC), lax.rem(t, Z * XC), h)
+        return (lax.div(t, Z * XC), lax.rem(t, Z * XC), h)
 
     loads = [
         pltpu.make_async_copy(tok_h, tok, load_sem.at[0]),
@@ -52,13 +52,15 @@
 
     barrier = pltpu.get_barrier_semaphore()
 
-    def greet(i, carry):
-        pl.semaphore_signal(
-            barrier, inc=1, device_id=device(lax.rem(me + i, N)), device_id_type=MESH
-        )
-        return carry
-
-    lax.fori_loop(1, N, greet, 0)
+    for dy in range(Y):
+        band = lax.rem(y + dy, Y)
+
+        def greet(i, carry):
+            to = (band, lax.rem(tk + i, Z * XC), h)
+            pl.semaphore_signal(barrier, inc=1, device_id=to, device_id_type=MESH)
+            return carry
+
+        lax.fori_loop(1 if dy == 0 else 0, Z * XC, greet, 0)
     pl.semaphore_signal(barrier, inc=1, device_id=other, device_id_type=MESH)
 
     out = lax.broadcasted_iota(jnp.int32, (256, 256), 0)
@@ -118,10 +120,6 @@
                         halo_hand(way, k).start()
                 halo_own(way).start()
 
-            @pl.when(xc != end)
-            def _():
-                halo_whole(way).start()
-
     def halo_forward():
         for way, _, _, end, _, _ in ways:
 
@@ -129,6 +127,7 @@
             def _():
                 pltpu.make_async_copy(relay.at[way], relay.at[way], hand_recv.at[way]).wait()
                 halo_pass(way).start()
+                halo_whole(way).start()
 
     def halo_got():
         for way, _, row, _, _, _ in ways:
@@ -155,6 +154,11 @@
             at = aligned(band * (Z * XC * CELL) + half * 256, 256)
             buf[pl.ds(at, 256), :] = dot(t1[...], stack).astype(BF16)
 
+    def offset(pair, which):
+        first = jnp.where(pair == 0, 0, jnp.where(pair == 1, 2, jnp.where(pair == 2, 3, 1)))
+        second = jnp.where(pair == 0, 4, jnp.where(pair == 1, 6, jnp.where(pair == 2, 5, 7)))
+        return jnp.where(which == 0, first, second), pair
+
     def send(dy, buf, dst, k, sems):
         band = lax.rem(y + dy, Y)
         mine = aligned(me * CELL, CELL)
@@ -165,21 +169,30 @@
                 buf.at[pl.ds(mine, CELL), :], dst.at[pl.ds(mine, CELL), :], sems(0)
             ).start()
 
-        def one(i, carry):
-            par = i // 16
-            dz = lax.rem(i // 4, 4) * 2 + par
-            t = band * (Z * XC) + lax.rem(z + dz, Z) * XC + lax.rem(xc + i, XC)
-            pltpu.make_async_remote_copy(
-                src_ref=buf.at[pl.ds(aligned(t * CELL, CELL), CELL), :],
-                dst_ref=dst.at[pl.ds(mine, CELL), :],
-                send_sem=send_sem.at[k],
-                recv_sem=sems(dy * 2 + par),
-                device_id=device(t),
-                device_id_type=MESH,
-            ).start()
+        def one(n, carry):
+            dz, group = offset(lax.div(n, 2), lax.rem(n, 2))
+            to_z = lax.rem(z + dz, Z)
+            for i in range(XC):
+                to = to_z * XC + lax.rem(xc + i, XC)
+
+                def go():
+                    at = aligned((band * (Z * XC) + to) * CELL, CELL)
+                    pltpu.make_async_remote_copy(
+                        src_ref=buf.at[pl.ds(at, CELL), :],
+                        dst_ref=dst.at[pl.ds(mine, CELL), :],
+                        send_sem=send_sem.at[k],
+                        recv_sem=sems(dy * 4 + group),
+                        device_id=(band, to, h),
+                        device_id_type=MESH,
+                    ).start()
+
+                if i == 0:
+                    pl.when(jnp.logical_or(dy > 0, n > 0))(go)
+                else:
+                    go()
             return carry
 
-        lax.fori_loop(jnp.where(dy == 0, 1, 0), Z * XC, one, 0)
+        lax.fori_loop(0, Z, one, 0)
 
     def wait_sent(buf, k):
         part = buf.at[pl.ds(0, (N - 1) * CELL), :]
@@ -206,8 +219,8 @@
 
     loads[0].wait()
     loads[1].wait()
-    loads[2].start()
-    loads[3].start()
+    for load in loads[2:]:
+        load.start()
 
     def mix_rows(dy, carry):
         band, cols = band_of(dy)
@@ -218,18 +231,19 @@
         send(dy, s1, r1, 0, lambda g: recv_sem.at[0])
         return carry
 
-    mix_rows(jnp.int32(0), 0)
-    send_rows(jnp.int32(0), 0)
-    halo_forward()
-
     def mix_and_send(dy, carry):
         mix_rows(dy, carry)
         return send_rows(dy, carry)
 
+    mix_and_send(jnp.int32(0), 0)
+    halo_forward()
     lax.fori_loop(1, Y, mix_and_send, 0)
 
     first, second, third = out >> 6, (out >> 2) & 15, out & 3
     t2[...] = (src == second * 16 + third * 4 + first).astype(F32).astype(BF16)
+    out, src = out[:128, :128], src[:128, :128]
+    first, second, third = out >> 5, (out >> 2) & 7, out & 3
+    t3[...] = (src == second * 16 + third * 4 + first).astype(F32).astype(BF16)
     cotp[:, 0:EDGE, :] = jnp.zeros((ROWS + 2, EDGE, SIZE), BF16)
     cotp[:, EDGE + SIZE :, :] = jnp.zeros((ROWS + 2, EDGE, SIZE), BF16)
     for i in range(3):
@@ -318,8 +332,11 @@
         )
         return carry
 
-    def send_back(dy, carry):
-        send(dy, s2, r4, 3, lambda g: last_sem.at[g])
+    def turn(i):
+        return i % 2 * 2 + i // 2 if isinstance(i, int) else lax.rem(i, 2) * 2 + lax.div(i, 2)
+
+    def send_back(i, carry):
+        send(turn(i), s2, r4, 3, lambda g: last_sem.at[g])
         return carry
 
     lax.fori_loop(0, Y, back_columns, 0)
@@ -443,29 +460,27 @@
                 row_done[q, part, :] = (terms[q] + row_got[q, part, :].astype(F32)).astype(BF16)
             row_store(base // BAND).start()
 
-    def arrive(dy, par):
+    def arrive(dy, pair):
         band, cols, away, base = source(dy)
-        g = dy * 2 + par
-        part = r4.at[pl.ds(0, 256), :]
-        pltpu.make_async_copy(part, part, last_sem.at[g]).wait()
-        zp = lax.rem(z + par, 2)
-        blocks = [r4[pl.ds(aligned((band * Z + zp + 2 * m) * 64, 64), 64), :] for m in range(4)]
-        block = dot(t2[...], jnp.concatenate(blocks, axis=0)).astype(BF16)
+        part = r4.at[pl.ds(0, 128), :]
+        pltpu.make_async_copy(part, part, last_sem.at[dy * 4 + pair]).wait()
+        zs = [lax.rem(z + Z - dz, Z) for dz in ((0, 4), (2, 6), (3, 5), (1, 7))[pair]]
+        blocks = [r4[pl.ds(aligned((band * Z + zz) * 64, 64), 64), :] for zz in zs]
+        block = dot(t3[...], jnp.concatenate(blocks, axis=0)).astype(BF16)
         for q in range(ROWS):
-            for m in range(4):
-                at = aligned(band * BAND + (zp + 2 * m) * 16, 16)
-                low = 64 * q + 16 * m
-                grows[q, pl.ds(at, 16), :] = block[low : low + 16]
+            for m, zz in enumerate(zs):
+                low = 32 * q + 16 * m
+                grows[q, pl.ds(aligned(band * BAND + zz * 16, 16), 16), :] = block[low : low + 16]
 
         @pl.when(away)
         def _():
             for q in range(ROWS):
-                term = dot(block[64 * q : 64 * q + 64], tok[q], ((1,), (1,))).astype(BF16)
-                for m in range(4):
-                    at = aligned(base + (zp + 2 * m) * 16, 16)
+                term = dot(block[32 * q : 32 * q + 32], tok[q], ((1,), (1,))).astype(BF16)
+                for m, zz in enumerate(zs):
+                    at = aligned(base + zz * 16, 16)
                     row_out[q, pl.ds(at, 16), :] = term[16 * m : 16 * m + 16]
-            for m in range(4):
-                row_copy(aligned(base + (zp + 2 * m) * 16, 16)).start()
+            for zz in zs:
+                row_copy(aligned(base + zz * 16, 16)).start()
 
     def back(dy, q):
         cols = source(dy)[1]
@@ -474,32 +489,33 @@
     def token_store(q):
         return pltpu.make_async_copy(mid.at[q], gtok_h.at[q], store_sem.at[ROWS + 2 + q])
 
-    for dy in range(Y):
-        arrive(dy, 0)
-        if dy == 3:
-            row_here(0)
-        arrive(dy, 1)
+    for i in range(Y):
+        dy = turn(i)
+        for pair in range(4):
+            arrive(dy, pair)
+            if i == 3 and pair == 0:
+                row_here(turn(0))
+            if i == 3 and pair == 1:
+                row_here(turn(1))
         for q in range(ROWS):
-            if dy < 3:
+            if i < 3:
                 hold[q] = back(dy, q)
             else:
                 mid[q] = back(dy, q).astype(BF16)
                 token_store(q).start()
-        if dy == 0:
+        if i == 0:
             lax.fori_loop(0, ROWS, column_here, 0)
-        if dy == 1:
+        if i == 1:
             sum_finish(0)
             sum_start(1)
-        if dy == 2:
+        if i == 2:
             sum_finish(1)
             sum_start(2)
-        if dy == 3:
-            row_here(1)
-            row_here(2)
-            sum_finish(2)
-            for i in range(3):
-                gkern[i] = total[3, 3 * i : 3 * i + 3, :]
-            row_here(3)
+    row_here(turn(2))
+    sum_finish(2)
+    for i in range(3):
+        gkern[i] = total[3, 3 * i : 3 * i + 3, :]
+    row_here(turn(3))
 
     wait_sent(s1, 2)
     wait_sent(s2, 3)
@@ -543,8 +559,8 @@
             vmem(half, BF16), vmem(half, BF16),
             vmem((2, SIZE // XC, SIZE), BF16), vmem((9, 8, SIZE), F32), vmem((16, SIZE), F32),
             vmem((4, 16, SIZE), F32), vmem((Z + Y + XC - 3, 16, SIZE), F32),
-            vmem((256, 256), BF16), vmem((256, 256), BF16),
-            dma((4,)), dma((2,)), dma((2,)), dma((2,)), dma((2,)), dma((2,)), dma((4,)), dma((3,)), dma((2 * Y,)),
+            vmem((256, 256), BF16), vmem((256, 256), BF16), vmem((128, 128), BF16),
+            dma((4,)), dma((2,)), dma((2,)), dma((2,)), dma((2,)), dma((2,)), dma((4,)), dma((3,)), dma((4 * Y,)),
             dma((ROWS,)), dma((ROWS,)), dma((2,)), dma((2,)), dma((3,)), dma((3,)),
             dma((2 * ROWS + 2,)),
         ],

time: 229 us -> 223 us (0.974)
  the two profiles are of different devices: /device:TPU:25 before, /device:TPU:1 now
where the time goes in v4:
time: 223 us
  Pallas kernels  218 us (98%)
  local copies, waits for them, and re-layouts  4.57 us (2%)
    pallas_call x1, Pallas kernels, shards(): pl.pallas_call(mixer, out_shape=[jax.ShapeDtypeStruct(full, BF16), jax.Sh...  218 us
    unnamed x6, local copies, waits for them, and re-layouts  4.57 us

profile of v4, /device:TPU:1, one launch (start us, length us, event | category | flops | bytes accessed | tf_op | source)
XLA Modules:
  0.0 223.2 jit_solution(15465169941275126509)
XLA Ops:
  0.6 0.0 copy-start
  0.6 0.7 copy-done
  1.3 217.9 %mixer.1 = (bf16[4,512,512]{2,1,0:T(8,128)(2,1)S(1)}, bf16[4,256,512]{2,1,0:T(8,128)(2,1)S(1)}, bf16[4,256,512]{2,1,0:T(8,128)(2,1)S(1)}, f32[3,3,512]{2,1,0:T(4,128)S(1)}) custom-call(bf16[4,512,512]{2,1,0:T(8,128)(2,1)} %tok_h.1, bf16[4,512,512]{2,1,0:T(8,128)(2,1)} %rf_h.1, bf16[4,512,512]{2,1,0:T(8,128)(2,1)} %cf_h.1, bf16[3,3,512]{2,1,0:T(4,128)(2,1)S(1)} %copy-done, ...), custom_call_target="tpu_custom_call" | custom-call | flops 7000000000 | bytes 12582912 | tf_op jit(solution)/shard_map/mixer/pallas_call | solution.py:542
  219.3 1.3 copy.13
  220.6 1.0 copy.14
  221.6 1.0 copy.15
  222.5 0.6 copy.16
Async XLA Ops:
  0.6 0.7 copy-start

commit v5 on v4

--- a/solution.py
+++ b/solution.py
@@ -157,39 +157,41 @@
     def offset(pair, which):
         first = jnp.where(pair == 0, 0, jnp.where(pair == 1, 2, jnp.where(pair == 2, 3, 1)))
         second = jnp.where(pair == 0, 4, jnp.where(pair == 1, 6, jnp.where(pair == 2, 5, 7)))
-        return jnp.where(which == 0, first, second), pair
-
-    def send(dy, buf, dst, k, sems):
-        band = lax.rem(y + dy, Y)
-        mine = aligned(me * CELL, CELL)
-
+        return jnp.where(which == 0, first, second)
+
+    def send_self(buf, dst, sem):
+        part = pl.ds(aligned(me * CELL, CELL), CELL)
+        pltpu.make_async_copy(buf.at[part, :], dst.at[part, :], sem).start()
+
+    def send_z(dy, dz, buf, dst, k, sem):
+        band, to_z = lax.rem(y + dy, Y), lax.rem(z + dz, Z)
+        for i in range(XC):
+            to = to_z * XC + lax.rem(xc + i, XC)
+
+            def go():
+                at = aligned((band * (Z * XC) + to) * CELL, CELL)
+                pltpu.make_async_remote_copy(
+                    src_ref=buf.at[pl.ds(at, CELL), :],
+                    dst_ref=dst.at[pl.ds(aligned(me * CELL, CELL), CELL), :],
+                    send_sem=send_sem.at[k],
+                    recv_sem=sem,
+                    device_id=(band, to, h),
+                    device_id_type=MESH,
+                ).start()
+
+            if i == 0:
+                pl.when(jnp.logical_or(dy > 0, dz > 0))(go)
+            else:
+                go()
+
+    def send(dy, buf, dst, k):
         @pl.when(dy == 0)
         def _():
-            pltpu.make_async_copy(
-                buf.at[pl.ds(mine, CELL), :], dst.at[pl.ds(mine, CELL), :], sems(0)
-            ).start()
+            send_self(buf, dst, recv_sem.at[k])
 
         def one(n, carry):
-            dz, group = offset(lax.div(n, 2), lax.rem(n, 2))
-            to_z = lax.rem(z + dz, Z)
-            for i in range(XC):
-                to = to_z * XC + lax.rem(xc + i, XC)
-
-                def go():
-                    at = aligned((band * (Z * XC) + to) * CELL, CELL)
-                    pltpu.make_async_remote_copy(
-                        src_ref=buf.at[pl.ds(at, CELL), :],
-                        dst_ref=dst.at[pl.ds(mine, CELL), :],
-                        send_sem=send_sem.at[k],
-                        recv_sem=sems(dy * 4 + group),
-                        device_id=(band, to, h),
-                        device_id_type=MESH,
-                    ).start()
-
-                if i == 0:
-                    pl.when(jnp.logical_or(dy > 0, n > 0))(go)
-                else:
-                    go()
+            dz = offset(lax.div(n, 2), lax.rem(n, 2))
+            send_z(dy, dz, buf, dst, k, recv_sem.at[k])
             return carry
 
         lax.fori_loop(0, Z, one, 0)
@@ -228,7 +230,7 @@
         return carry
 
     def send_rows(dy, carry):
-        send(dy, s1, r1, 0, lambda g: recv_sem.at[0])
+        send(dy, s1, r1, 0)
         return carry
 
     def mix_and_send(dy, carry):
@@ -301,7 +303,7 @@
     def send_grad(dy, carry):
         band, cols = band_of(dy)
         pack(band, [mid[q, cols, :] for q in range(ROWS)], s2)
-        send(dy, s2, r2, 1, lambda g: recv_sem.at[1])
+        send(dy, s2, r2, 1)
         return carry
 
     lax.fori_loop(0, Y, send_grad, 0)
@@ -314,7 +316,7 @@
     def mix_columns(dy, carry):
         band, cols = band_of(dy)
         pack(band, [dot(cf[q, cols, :], xs[q]).astype(BF16) for q in range(ROWS)], s1)
-        send(dy, s1, r3, 2, lambda g: recv_sem.at[2])
+        send(dy, s1, r3, 2)
         return carry
 
     lax.fori_loop(0, Y, mix_columns, 0)
@@ -332,15 +334,24 @@
         )
         return carry
 
-    def turn(i):
-        return i % 2 * 2 + i // 2 if isinstance(i, int) else lax.rem(i, 2) * 2 + lax.div(i, 2)
+    def group(i):
+        dy = lax.rem(i, 2) * 2 + lax.div(lax.rem(i, 4), 2)
+        late = 2 + lax.rem(1 + i + lax.div(i, 4), 2)
+        return dy, jnp.where(i < 8, lax.div(i, 4), late)
 
     def send_back(i, carry):
-        send(turn(i), s2, r4, 3, lambda g: last_sem.at[g])
+        dy, pair = group(i)
+
+        @pl.when(i == 0)
+        def _():
+            send_self(s2, r4, last_sem.at[0])
+
+        for which in range(2):
+            send_z(dy, offset(pair, which), s2, r4, 3, last_sem.at[i])
         return carry
 
     lax.fori_loop(0, Y, back_columns, 0)
-    lax.fori_loop(0, Y // 2, send_back, 0)
+    lax.fori_loop(0, 8, send_back, 0)
 
     def half_of(which):
         return pl.ds(aligned(which * (SIZE // 2), SIZE // 2), SIZE // 2)
@@ -413,7 +424,7 @@
     for k in range(9):
         total[0, k : k + 1, :] = jnp.sum(taps[k], axis=0, keepdims=True)
     sum_start(0)
-    lax.fori_loop(Y // 2, Y, send_back, 0)
+    lax.fori_loop(8, 16, send_back, 0)
 
     def column_store(q):
         return pltpu.make_async_copy(col_done.at[q], gcol_h.at[q], store_sem.at[q])
@@ -460,10 +471,12 @@
                 row_done[q, part, :] = (terms[q] + row_got[q, part, :].astype(F32)).astype(BF16)
             row_store(base // BAND).start()
 
-    def arrive(dy, pair):
+    def arrive(i):
+        dy = i % 2 * 2 + i % 4 // 2
+        pair = i // 4 if i < 8 else 2 + (1 + i + i // 4) % 2
         band, cols, away, base = source(dy)
         part = r4.at[pl.ds(0, 128), :]
-        pltpu.make_async_copy(part, part, last_sem.at[dy * 4 + pair]).wait()
+        pltpu.make_async_copy(part, part, last_sem.at[i]).wait()
         zs = [lax.rem(z + Z - dz, Z) for dz in ((0, 4), (2, 6), (3, 5), (1, 7))[pair]]
         blocks = [r4[pl.ds(aligned((band * Z + zz) * 64, 64), 64), :] for zz in zs]
         block = dot(t3[...], jnp.concatenate(blocks, axis=0)).astype(BF16)
@@ -482,40 +495,41 @@
             for zz in zs:
                 row_copy(aligned(base + zz * 16, 16)).start()
 
-    def back(dy, q):
-        cols = source(dy)[1]
-        return hold[q] + dot(rf[q, cols, :], grows[q, cols, :], ((0,), (0,)))
+    def back(par, q):
+        zp = lax.rem(z + par, 2)
+        parts = [
+            pl.ds(aligned(band * BAND + (zp + 2 * m) * 16, 16), 16)
+            for band in range(Y)
+            for m in range(Z // 2)
+        ]
+        factor = jnp.concatenate([rf[q, part, :] for part in parts], axis=0)
+        grads = jnp.concatenate([grows[q, part, :] for part in parts], axis=0)
+        return hold[q] + dot(factor, grads, ((0,), (0,)))
 
     def token_store(q):
         return pltpu.make_async_copy(mid.at[q], gtok_h.at[q], store_sem.at[ROWS + 2 + q])
 
-    for i in range(Y):
-        dy = turn(i)
-        for pair in range(4):
-            arrive(dy, pair)
-            if i == 3 and pair == 0:
-                row_here(turn(0))
-            if i == 3 and pair == 1:
-                row_here(turn(1))
-        for q in range(ROWS):
-            if i < 3:
-                hold[q] = back(dy, q)
-            else:
-                mid[q] = back(dy, q).astype(BF16)
-                token_store(q).start()
-        if i == 0:
+    for i in range(16):
+        arrive(i)
+        if i == 3:
             lax.fori_loop(0, ROWS, column_here, 0)
-        if i == 1:
+        if i == 7:
+            for q in range(ROWS):
+                hold[q] = back(0, q)
+        if i == 8:
             sum_finish(0)
             sum_start(1)
-        if i == 2:
+        if i == 12:
             sum_finish(1)
             sum_start(2)
-    row_here(turn(2))
+    for q in range(ROWS):
+        mid[q] = back(1, q).astype(BF16)
+        token_store(q).start()
     sum_finish(2)
     for i in range(3):
         gkern[i] = total[3, 3 * i : 3 * i + 3, :]
-    row_here(turn(3))
+    for dy in range(Y):
+        row_here(dy)
 
     wait_sent(s1, 2)
     wait_sent(s2, 3)

time: 223 us -> 219 us (0.982)
  Pallas kernels: 218 us -> 214 us
    pallas_call x1, Pallas kernels: 218 us -> 214 us  [shards(): pl.pallas_call(mixer, out_shape=[jax.ShapeDtypeStruct(full, BF16), jax.Sh...]
where the time goes in v5:
time: 219 us
  Pallas kernels  214 us (98%)
  local copies, waits for them, and re-layouts  4.57 us (2%)
    pallas_call x1, Pallas kernels, shards(): pl.pallas_call(mixer, out_shape=[jax.ShapeDtypeStruct(full, BF16), jax.Sh...  214 us
    unnamed x6, local copies, waits for them, and re-layouts  4.57 us

profile of v5, /device:TPU:1, one launch (start us, length us, event | category | flops | bytes accessed | tf_op | source)
XLA Modules:
  0.0 219.2 jit_solution(18409038418329341961)
XLA Ops:
  0.6 0.0 copy-start
  0.6 0.7 copy-done
  1.3 214.0 %mixer.1 = (bf16[4,512,512]{2,1,0:T(8,128)(2,1)S(1)}, bf16[4,256,512]{2,1,0:T(8,128)(2,1)S(1)}, bf16[4,256,512]{2,1,0:T(8,128)(2,1)S(1)}, f32[3,3,512]{2,1,0:T(4,128)S(1)}) custom-call(bf16[4,512,512]{2,1,0:T(8,128)(2,1)} %tok_h.1, bf16[4,512,512]{2,1,0:T(8,128)(2,1)} %rf_h.1, bf16[4,512,512]{2,1,0:T(8,128)(2,1)} %cf_h.1, bf16[3,3,512]{2,1,0:T(4,128)(2,1)S(1)} %copy-done, ...), custom_call_target="tpu_custom_call" | custom-call | flops 7000000000 | bytes 12582912 | tf_op jit(solution)/shard_map/mixer/pallas_call | solution.py:556
  215.4 1.3 copy.13
  216.7 1.0 copy.14
  217.7 1.0 copy.15
  218.6 0.6 copy.16
Async XLA Ops:
  0.6 0.7 copy-start

commit v6 on v5

--- a/solution.py
+++ b/solution.py
@@ -546,7 +546,30 @@
         token_store(q).wait()
 
 
+def hand_out(tok_v, row_v, col_v, kern_v, tok_h, row_h, col_h, kern_h, sems):
+    pairs = ((tok_v, tok_h), (row_v, row_h), (col_v, col_h), (kern_v, kern_h))
+    copies = [pltpu.make_async_copy(a, b, sems.at[i]) for i, (a, b) in enumerate(pairs)]
+    for copy in copies:
+        copy.start()
+    for copy in copies:
+        copy.wait()
+
+
 def shards(tokens, row_factor, column_factor, kernel, cotangent):
+    whole = pl.BlockSpec(memory_space=pl.ANY)
+    results = compute(tokens, row_factor, column_factor, kernel, cotangent)
+    return pl.pallas_call(
+        hand_out,
+        out_shape=[jax.ShapeDtypeStruct(r.shape, r.dtype) for r in results],
+        in_specs=[whole] * 4,
+        out_specs=[whole] * 4,
+        scratch_shapes=[pltpu.SemaphoreType.DMA((4,))],
+        name="hand_out",
+        compiler_params=pltpu.CompilerParams(vmem_limit_bytes=2**20),
+    )(*results)
+
+
+def compute(tokens, row_factor, column_factor, kernel, cotangent):
     full = (ROWS, SIZE, SIZE)
     half = (ROWS, SIZE // 2, SIZE)
     flat = (N * CELL, SIZE)

time: 219 us -> 218 us (level)
  local copies, waits for them, and re-layouts: 4.57 us -> 0.7 us
    unnamed x6 -> x2, local copies, waits for them, and re-layouts: 4.57 us -> 0.7 us
    pallas_call x1 -> x2, Pallas kernels: 214 us -> 216 us  [the longest x1 214 us: compute(): pl.pallas_call(mixer, out_shape=[jax.ShapeDtypeStruct(full, BF16), jax.Sh...]
where the time goes in v6:
time: 218 us; the launch traced here: 217 us
  Pallas kernels  216 us (99%)
    pallas_call x1, Pallas kernels, compute(): pl.pallas_call(mixer, out_shape=[jax.ShapeDtypeStruct(full, BF16), jax.Sh...  214 us

profile of v6, /device:TPU:1, one launch (start us, length us, event | category | flops | bytes accessed | tf_op | source)
XLA Modules:
  0.0 217.4 jit_solution(2020097914184111670)
XLA Ops:
  0.6 0.0 copy-start
  0.6 0.7 copy-done
  1.3 214.0 %mixer.1 = (bf16[4,512,512]{2,1,0:T(8,128)(2,1)S(1)}, bf16[4,256,512]{2,1,0:T(8,128)(2,1)S(1)}, bf16[4,256,512]{2,1,0:T(8,128)(2,1)S(1)}, f32[3,3,512]{2,1,0:T(4,128)S(1)}) custom-call(bf16[4,512,512]{2,1,0:T(8,128)(2,1)} %tok_h.1, bf16[4,512,512]{2,1,0:T(8,128)(2,1)} %rf_h.1, bf16[4,512,512]{2,1,0:T(8,128)(2,1)} %cf_h.1, bf16[3,3,512]{2,1,0:T(4,128)(2,1)S(1)} %copy-done, ...), custom_call_target="tpu_custom_call" | custom-call | flops 7000000000 | bytes 12582912 | tf_op jit(solution)/shard_map/mixer/pallas_call | solution.py:579
  215.4 2.0 hand_out.1
Async XLA Ops:
  0.6 0.7 copy-start

commit v7 on v6

--- a/solution.py
+++ b/solution.py
@@ -56,11 +56,19 @@
         band = lax.rem(y + dy, Y)
 
         def greet(i, carry):
-            to = (band, lax.rem(tk + i, Z * XC), h)
-            pl.semaphore_signal(barrier, inc=1, device_id=to, device_id_type=MESH)
+            for k in range(XC):
+                to = (band, i * XC + k, h)
+                if dy == 0:
+
+                    @pl.when(i * XC + k != tk)
+                    def _():
+                        pl.semaphore_signal(barrier, inc=1, device_id=to, device_id_type=MESH)
+
+                else:
+                    pl.semaphore_signal(barrier, inc=1, device_id=to, device_id_type=MESH)
             return carry
 
-        lax.fori_loop(1 if dy == 0 else 0, Z * XC, greet, 0)
+        lax.fori_loop(0, Z, greet, 0)
     pl.semaphore_signal(barrier, inc=1, device_id=other, device_id_type=MESH)
 
     out = lax.broadcasted_iota(jnp.int32, (256, 256), 0)
@@ -528,7 +536,7 @@
     sum_finish(2)
     for i in range(3):
         gkern[i] = total[3, 3 * i : 3 * i + 3, :]
-    for dy in range(Y):
+    for dy in (0, 2, 1, 3):
         row_here(dy)
 
     wait_sent(s1, 2)

time: 218 us -> 217 us (level)
  no operation moved by 1% of the time
where the time goes in v7:
time: 217 us
  Pallas kernels  216 us (100%)
    pallas_call x1, Pallas kernels, compute(): pl.pallas_call(mixer, out_shape=[jax.ShapeDtypeStruct(full, BF16), jax.Sh...  214 us

profile of v7, /device:TPU:1, one launch (start us, length us, event | category | flops | bytes accessed | tf_op | source)
XLA Modules:
  0.0 217.1 jit_solution(13652396597606879051)
XLA Ops:
  0.6 0.0 copy-start
  0.6 0.7 copy-done
  1.3 213.6 %mixer.1 = (bf16[4,512,512]{2,1,0:T(8,128)(2,1)S(1)}, bf16[4,256,512]{2,1,0:T(8,128)(2,1)S(1)}, bf16[4,256,512]{2,1,0:T(8,128)(2,1)S(1)}, f32[3,3,512]{2,1,0:T(4,128)S(1)}) custom-call(bf16[4,512,512]{2,1,0:T(8,128)(2,1)} %tok_h.1, bf16[4,512,512]{2,1,0:T(8,128)(2,1)} %rf_h.1, bf16[4,512,512]{2,1,0:T(8,128)(2,1)} %cf_h.1, bf16[3,3,512]{2,1,0:T(4,128)(2,1)S(1)} %copy-done, ...), custom_call_target="tpu_custom_call" | custom-call | flops 7000000000 | bytes 12582912 | tf_op jit(solution)/shard_map/mixer/pallas_call | solution.py:587
  214.9 2.0 hand_out.1
Async XLA Ops:
  0.6 0.7 copy-start
